TPU v7x, 32 devices: a whole 2x2x4 slice. The times are simulated.
32 devices in a mesh: gene: 8 (over z, y), cell: 4 (over x, core).
Axes of the slice: x: 2, y: 2, z: 4, core: 2. Of those that a mesh axis runs over, the one named last changes fastest.
Arguments:
- counts: bfloat16 [4096, 1792], P('cell', 'gene'), may hold values from -12 to 12
- study: int32 [4096], P('cell'), may hold values from 0 to 7
- study_gene_mask: int32 [8, 1792], P(None, 'gene'), may hold values 0 or 1
- noise: float32 [4096, 100], P(('cell', 'gene')), may hold values from -5 to 5
- enc_in: float32 [1792, 800], P('gene'), may hold values from -0.125 to 0.125
- enc_mid: float32 [800, 800], replicated, may hold values from -0.21875 to 0.21875
- latent_w: float32 [2, 800, 100], replicated, may hold values from -0.21875 to 0.21875
- dec_in: float32 [100, 800], replicated, may hold values from -0.625 to 0.625
- dec_mid: float32 [800, 800], replicated, may hold values from -0.21875 to 0.21875
- dec_out: float32 [800, 1792], P(None, 'gene'), may hold values from -0.21875 to 0.21875
- norm_params: float32 [2, 4, 800], replicated, may hold values from 0.5 to 1.5
- latent_bias: float32 [2, 100], replicated, may hold values from -3 to 3
- out_bias: float32 [1792], P('gene'), may hold values from -3 to 3
- running_mean: float32 [4, 800], replicated, may hold values from -3 to 3
- running_variance: float32 [4, 800], replicated, may hold values from 0.5 to 4
- mom_enc_in: float32 [1792, 800], P('gene'), may hold values from -1.5 to 1.5
- mom_enc_mid: float32 [800, 800], replicated, may hold values from -0.75 to 0.75
- mom_latent_w: float32 [2, 800, 100], replicated, may hold values from -2 to 2
- mom_dec_in: float32 [100, 800], replicated, may hold values from -0.75 to 0.75
- mom_dec_mid: float32 [800, 800], replicated, may hold values from -0.75 to 0.75
- mom_dec_out: float32 [800, 1792], P(None, 'gene'), may hold values from -0.5 to 0.5
- mom_norm: float32 [2, 4, 800], replicated, may hold values from -0.75 to 0.75
- mom_latent_bias: float32 [2, 100], replicated, may hold values from -2 to 2
- mom_out_bias: float32 [1792], P('gene'), may hold values from -1 to 1
Outputs:
- recon: bfloat16 [4096, 1792], P('cell', 'gene')
- loss: float32 [], replicated
- new_enc_in: float32 [1792, 800], P('gene')
- new_mom_enc_in: float32 [1792, 800], P('gene')
- new_enc_mid: float32 [800, 800], replicated
- new_mom_enc_mid: float32 [800, 800], replicated
- new_latent_w: float32 [2, 800, 100], replicated
- new_mom_latent_w: float32 [2, 800, 100], replicated
- new_dec_in: float32 [100, 800], replicated
- new_mom_dec_in: float32 [100, 800], replicated
- new_dec_mid: float32 [800, 800], replicated
- new_mom_dec_mid: float32 [800, 800], replicated
- new_dec_out: float32 [800, 1792], P(None, 'gene')
- new_mom_dec_out: float32 [800, 1792], P(None, 'gene')
- new_norm_params: float32 [2, 4, 800], replicated
- new_mom_norm: float32 [2, 4, 800], replicated
- new_latent_bias: float32 [2, 100], replicated
- new_mom_latent_bias: float32 [2, 100], replicated
- new_out_bias: float32 [1792], P('gene')
- new_mom_out_bias: float32 [1792], P('gene')
- new_running_mean: float32 [4, 800], replicated
- updated_running_variance: float32 [4, 800], replicated
All inputs are finite; a program needn't handle non-finite values. No bound on the sum of `study_gene_mask` on one device may be relied on, other than what follows from the above.
Results may differ from a plain program's by a relative error of at most 0.013.
Values may be sent and summed in bfloat16 or wider, within the bound.
No kernel may reach another device: no remote copies, remote signals or barrier semaphores. Data moves between devices by JAX's collectives and lax.ppermute only.
A program may use at most 192 MiB of HBM per device.

v0:
```python
import math

import jax
import jax.numpy as jnp
from jax import lax
from jax.sharding import PartitionSpec as P

NS = 5


EPSILON = 1e-05
ALPHA_KL = 5e-05
MOMENTUM = 0.95
RATE = 0.5
RATE_VECTOR = 0.2
COEF_A = 3.4445
COEF_B = -4.775
COEF_C = 2.0315
HIGH = lax.Precision.HIGHEST


def matmul(left, right):
    return jnp.dot(left, right, precision=HIGH, preferred_element_type=jnp.float32)


def inner_rows(left, right):
    return lax.dot_general(
        left, right, (((0,), (0,)), ((), ())), preferred_element_type=jnp.float32
    )


def outer_cols(left, right):
    return lax.dot_general(
        left, right, (((1,), (1,)), ((), ())), preferred_element_type=jnp.float32
    )


def normalize(values, norm_params, layer, cells):
    totals = lax.psum((jnp.sum(values, axis=0), jnp.sum(values * values, axis=0)), ("gene", "cell"))
    batch_mean = totals[0] / cells
    batch_var = totals[1] / cells - batch_mean * batch_mean
    inverse = lax.rsqrt(batch_var + EPSILON)
    scaled = (values - batch_mean) * inverse
    shifted = scaled * norm_params[0, layer] + norm_params[1, layer]
    return (jax.nn.gelu(shifted), (shifted, scaled, inverse, batch_mean, batch_var))


def norm_back(grad_out, saved, norm_params, layer, cells):
    shifted, scaled, inverse = (saved[0], saved[1], saved[2])
    unused, pullback = jax.vjp(jax.nn.gelu, shifted)
    grad_shift = pullback(grad_out)[0]
    sums = lax.psum(
        (jnp.sum(grad_shift, axis=0), jnp.sum(grad_shift * scaled, axis=0)), ("gene", "cell")
    )
    grad_in = (
        norm_params[0, layer] * inverse * (grad_shift - sums[0] / cells - scaled * sums[1] / cells)
    )
    return (grad_in.astype(jnp.bfloat16), sums[1], sums[0])


def orthogonal(moment):
    current = moment / (jnp.sqrt(jnp.sum(moment * moment)) + 1e-07)
    incoming_rows, cols_out = moment.shape
    for iteration in range(NS):
        if incoming_rows >= cols_out:
            gram = matmul(current.T, current)
            current = COEF_A * current + matmul(
                current, COEF_B * gram + COEF_C * matmul(gram, gram)
            )
        else:
            gram = matmul(current, current.T)
            current = COEF_A * current + matmul(
                COEF_B * gram + COEF_C * matmul(gram, gram), current
            )
    return current


def vector_step(value, moment, square):
    return value - RATE_VECTOR * moment * lax.rsqrt(square + 1e-06)


def shards(
    counts,
    study,
    study_gene_mask,
    noise,
    enc_in,
    enc_mid,
    latent_w,
    dec_in,
    dec_mid,
    dec_out,
    norm_params,
    latent_bias,
    out_bias,
    running_mean,
    running_variance,
    mom_enc_in,
    mom_enc_mid,
    mom_latent_w,
    mom_dec_in,
    mom_dec_mid,
    mom_dec_out,
    mom_norm,
    mom_latent_bias,
    mom_out_bias,
):
    gene_count = lax.axis_size("gene")
    cell_count = lax.axis_size("cell")
    group_rows, gene_local = counts.shape
    cells = group_rows * cell_count
    genes = gene_local * gene_count
    hidden_width = enc_mid.shape[0]
    study_labels = study_gene_mask.shape[0]
    selection_matrix = (
        study[:, None] == jnp.arange(study_labels, dtype=jnp.int32)[None, :]
    ).astype(jnp.float32)
    gene_mask = jnp.dot(selection_matrix, study_gene_mask.astype(jnp.float32))
    encoder_input_reduced = enc_in.astype(jnp.bfloat16)
    enc_mid_low = enc_mid.astype(jnp.bfloat16)
    latent_low = latent_w.astype(jnp.bfloat16)
    dec_in_low = dec_in.astype(jnp.bfloat16)
    dec_mid_low = dec_mid.astype(jnp.bfloat16)
    dec_out_low = dec_out.astype(jnp.bfloat16)
    block = counts
    first = lax.psum_scatter(
        jnp.dot(block, encoder_input_reduced, preferred_element_type=jnp.float32),
        "gene",
        scatter_dimension=0,
        tiled=True,
    )
    hidden_one, saved_one = normalize(first, norm_params, 0, cells)
    one_low = hidden_one.astype(jnp.bfloat16)
    second = jnp.dot(one_low, enc_mid_low, preferred_element_type=jnp.float32)
    hidden_two, saved_two = normalize(second, norm_params, 1, cells)
    two_low = hidden_two.astype(jnp.bfloat16)
    latent_mean = (
        jnp.dot(two_low, latent_low[0], preferred_element_type=jnp.float32) + latent_bias[0]
    )
    latent_logvar = (
        jnp.dot(two_low, latent_low[1], preferred_element_type=jnp.float32) + latent_bias[1]
    )
    spread_factor = jnp.exp(0.5 * latent_logvar)
    sample_low = (latent_mean + noise * spread_factor).astype(jnp.bfloat16)
    third = jnp.dot(sample_low, dec_in_low, preferred_element_type=jnp.float32)
    hidden_three, saved_three = normalize(third, norm_params, 2, cells)
    three_low = hidden_three.astype(jnp.bfloat16)
    fourth = jnp.dot(three_low, dec_mid_low, preferred_element_type=jnp.float32)
    hidden_four, saved_four = normalize(fourth, norm_params, 3, cells)
    four_low = hidden_four.astype(jnp.bfloat16)
    all_four = lax.all_gather(four_low, "gene", axis=0, tiled=True)
    decoded = jnp.dot(all_four, dec_out_low, preferred_element_type=jnp.float32) + out_bias
    error = decoded - counts.astype(jnp.float32)
    loss_part = 0.5 / genes * jnp.sum(gene_mask * error * error)
    kl_scale = ALPHA_KL / genes
    loss_part = loss_part + kl_scale * 0.5 * jnp.sum(
        jnp.exp(latent_logvar) + latent_mean * latent_mean - 1.0 - latent_logvar
    )
    grad_decoded = (gene_mask * error / genes).astype(jnp.bfloat16)
    grad_out_bias = jnp.sum(grad_decoded, axis=0, dtype=jnp.float32)
    grad_dec_out = inner_rows(all_four, grad_decoded)
    block = grad_decoded
    grad_four = lax.psum_scatter(
        outer_cols(block, dec_out_low), "gene", scatter_dimension=0, tiled=True
    )
    grad_a4, gain_four, shift_four = norm_back(grad_four, saved_four, norm_params, 3, cells)
    decoder_middle_gradient = inner_rows(three_low, grad_a4)
    grad_three = outer_cols(grad_a4, dec_mid_low)
    grad_a3, gain_three, shift_three = norm_back(grad_three, saved_three, norm_params, 2, cells)
    grad_dec_in = inner_rows(sample_low, grad_a3)
    grad_sample = outer_cols(grad_a3, dec_in_low)
    grad_mean = (grad_sample + kl_scale * latent_mean).astype(jnp.bfloat16)
    grad_logvar = (
        grad_sample * noise * 0.5 * spread_factor + kl_scale * 0.5 * (jnp.exp(latent_logvar) - 1.0)
    ).astype(jnp.bfloat16)
    grad_latent_bias = jnp.stack(
        [
            jnp.sum(grad_mean, axis=0, dtype=jnp.float32),
            jnp.sum(grad_logvar, axis=0, dtype=jnp.float32),
        ]
    )
    grad_latent_w = jnp.stack([inner_rows(two_low, grad_mean), inner_rows(two_low, grad_logvar)])
    grad_two = outer_cols(grad_mean, latent_low[0]) + outer_cols(grad_logvar, latent_low[1])
    grad_a2, gain_two, shift_two = norm_back(grad_two, saved_two, norm_params, 1, cells)
    grad_enc_mid = inner_rows(one_low, grad_a2)
    grad_one = outer_cols(grad_a2, enc_mid_low)
    grad_a1, gain_one, shift_one = norm_back(grad_one, saved_one, norm_params, 0, cells)
    block = counts
    grad_enc_in = inner_rows(block, lax.all_gather(grad_a1, "gene", axis=0, tiled=True))
    grad_norm = jnp.stack(
        [
            jnp.stack([gain_one, gain_two, gain_three, gain_four]),
            jnp.stack([shift_one, shift_two, shift_three, shift_four]),
        ]
    )
    grad_enc_in, grad_dec_out, grad_out_bias = lax.psum(
        (grad_enc_in, grad_dec_out, grad_out_bias), "cell"
    )
    grad_enc_mid, grad_latent_w, grad_dec_in, decoder_middle_gradient, grad_latent_bias, total = (
        lax.psum(
            (
                grad_enc_mid,
                grad_latent_w,
                grad_dec_in,
                decoder_middle_gradient,
                grad_latent_bias,
                loss_part,
            ),
            ("gene", "cell"),
        )
    )
    new_mom_enc_in = MOMENTUM * mom_enc_in + grad_enc_in
    new_mom_dec_out = MOMENTUM * mom_dec_out + grad_dec_out
    new_mom_out_bias = MOMENTUM * mom_out_bias + grad_out_bias
    square_in, square_out, square_bias = lax.psum(
        (
            jnp.sum(new_mom_enc_in * new_mom_enc_in),
            jnp.sum(new_mom_dec_out * new_mom_dec_out),
            jnp.sum(new_mom_out_bias * new_mom_out_bias),
        ),
        "gene",
    )
    tall = new_mom_enc_in / (jnp.sqrt(square_in) + 1e-07)
    wide = new_mom_dec_out / (jnp.sqrt(square_out) + 1e-07)
    for iteration in range(NS):
        gram = jnp.stack([matmul(tall.T, tall), matmul(wide, wide.T)])
        shares = lax.psum_scatter(gram, "gene", scatter_dimension=1, tiled=True)
        whole = lax.all_gather(shares, "gene", axis=1, tiled=True)
        polynom = COEF_B * whole + COEF_C * jnp.einsum("bij,bjk->bik", whole, whole, precision=HIGH)
        tall = COEF_A * tall + matmul(tall, polynom[0])
        wide = COEF_A * wide + matmul(polynom[1], wide)
    new_enc_in = enc_in - RATE * math.sqrt(max(1.0, hidden_width / genes)) * tall
    new_dec_out = dec_out - RATE * math.sqrt(max(1.0, genes / hidden_width)) * wide
    new_out_bias = vector_step(out_bias, new_mom_out_bias, square_bias / genes)
    new_mom_enc_mid = MOMENTUM * mom_enc_mid + grad_enc_mid
    new_mom_latent_w = MOMENTUM * mom_latent_w + grad_latent_w
    new_mom_dec_in = MOMENTUM * mom_dec_in + grad_dec_in
    new_mom_dec_mid = MOMENTUM * mom_dec_mid + decoder_middle_gradient
    weights = [enc_mid, latent_w[0], latent_w[1], dec_in, dec_mid]
    moments = [
        new_mom_enc_mid,
        new_mom_latent_w[0],
        new_mom_latent_w[1],
        new_mom_dec_in,
        new_mom_dec_mid,
    ]
    results = []
    for number in range(5):
        results.append(orthogonal(moments[number]))
    updated = []
    for number in range(5):
        factor = math.sqrt(max(1.0, weights[number].shape[1] / weights[number].shape[0]))
        updated.append(weights[number] - RATE * factor * results[number])
    new_mom_norm = MOMENTUM * mom_norm + grad_norm
    new_norm = vector_step(
        norm_params, new_mom_norm, jnp.mean(new_mom_norm * new_mom_norm, axis=-1, keepdims=True)
    )
    new_mom_latent_bias = MOMENTUM * mom_latent_bias + grad_latent_bias
    new_latent_bias = vector_step(
        latent_bias,
        new_mom_latent_bias,
        jnp.mean(new_mom_latent_bias * new_mom_latent_bias, axis=-1, keepdims=True),
    )
    means = jnp.stack([saved_one[3], saved_two[3], saved_three[3], saved_four[3]])
    variances = jnp.stack([saved_one[4], saved_two[4], saved_three[4], saved_four[4]])
    new_running_mean = 0.9 * running_mean + 0.1 * means
    updated_running_variance = 0.9 * running_variance + 0.1 * variances * (cells / (cells - 1.0))
    return (
        decoded.astype(jnp.bfloat16),
        total / cells,
        new_enc_in,
        new_mom_enc_in,
        updated[0],
        new_mom_enc_mid,
        jnp.stack([updated[1], updated[2]]),
        new_mom_latent_w,
        updated[3],
        new_mom_dec_in,
        updated[4],
        new_mom_dec_mid,
        new_dec_out,
        new_mom_dec_out,
        new_norm,
        new_mom_norm,
        new_latent_bias,
        new_mom_latent_bias,
        new_out_bias,
        new_mom_out_bias,
        new_running_mean,
        updated_running_variance,
    )


def solution(mesh):
    in_specs = (
        P("cell", "gene"),
        P("cell"),
        P(None, "gene"),
        P(("cell", "gene"), None),
        P("gene", None),
        P(),
        P(),
        P(),
        P(),
        P(None, "gene"),
        P(),
        P(),
        P("gene"),
        P(),
        P(),
        P("gene", None),
        P(),
        P(),
        P(),
        P(),
        P(None, "gene"),
        P(),
        P(),
        P("gene"),
    )
    out_specs = (
        P("cell", "gene"),
        P(),
        P("gene", None),
        P("gene", None),
        P(),
        P(),
        P(),
        P(),
        P(),
        P(),
        P(),
        P(),
        P(None, "gene"),
        P(None, "gene"),
        P(),
        P(),
        P(),
        P(),
        P("gene"),
        P("gene"),
        P(),
        P(),
    )
    return jax.shard_map(shards, mesh=mesh, in_specs=in_specs, out_specs=out_specs, check_vma=False)
```

profile of v0, /device:TPU:0, one launch (start us, length us, event | category | flops | bytes accessed | tf_op | source)
XLA Modules:
  0.0 2634.5 jit_solution(6115569375105480803)
XLA Ops:
  14.2 76.7 %reduce-scatter.3.cloned.1.call-done = f32[128,800]{0,1:T(8,128)} async-done(((f32[1024,800]{0,1:T(8,128)}), f32[128,800]{0,1:T(8,128)}) %reduce-scatter.3.cloned.1.call-update) | async-done | bytes 409616 | tf_op jit(solution)/shard_map/reduce_scatter | solution.py:126
  92.2 39.8 %all-reduce.12 = (f32[800]{0:T(1024)S(1)}, f32[800]{0:T(1024)S(1)}) all-reduce(f32[800]{0:T(1024)S(1)} %get-tuple-element.107, f32[800]{0:T(1024)S(1)} %get-tuple-element.106), channel_id=1, replica_groups=mesh['gene'=8,'cell'=4] {'gene','cell'}, use_global_device_ids=true, to_apply=%region_4.0 | all-reduce | flops 1600 | bytes 12800 | tf_op jit(solution)/shard_map/psum | solution.py:39
  135.1 39.6 %all-reduce.11 = (f32[800]{0:T(1024)S(1)}, f32[800]{0:T(1024)S(1)}) all-reduce(f32[800]{0:T(1024)S(1)} %get-tuple-element.105, f32[800]{0:T(1024)S(1)} %get-tuple-element.104), channel_id=1, replica_groups=mesh['gene'=8,'cell'=4] {'gene','cell'}, use_global_device_ids=true, to_apply=%region_8.0 | all-reduce | flops 1600 | bytes 12800 | tf_op jit(solution)/shard_map/psum | solution.py:39
  182.1 40.8 %all-reduce.10 = (f32[800]{0:T(1024)}, f32[800]{0:T(1024)}) all-reduce(f32[800]{0:T(1024)} %get-tuple-element.103, f32[800]{0:T(1024)S(1)} %get-tuple-element.102), channel_id=1, replica_groups=mesh['gene'=8,'cell'=4] {'gene','cell'}, use_global_device_ids=true, to_apply=%region_12.0 | all-reduce | flops 1600 | bytes 12800 | tf_op jit(solution)/shard_map/psum | solution.py:39
  229.2 40.1 %all-reduce.9 = (f32[800]{0:T(1024)}, f32[800]{0:T(1024)}) all-reduce(f32[800]{0:T(1024)} %get-tuple-element.101, f32[800]{0:T(1024)} %get-tuple-element.100), channel_id=1, replica_groups=mesh['gene'=8,'cell'=4] {'gene','cell'}, use_global_device_ids=true, to_apply=%region_16.0 | all-reduce | flops 1600 | bytes 12800 | tf_op jit(solution)/shard_map/psum | solution.py:39
  274.1 46.3 %all-gather.8.cloned.1.call-done = bf16[1024,800]{0,1:T(8,128)(2,1)} async-done(((bf16[128,800]{0,1:T(8,128)(2,1)}), bf16[1024,800]{0,1:T(8,128)(2,1)}) %all-gather.8.cloned.1.call-update) | async-done | bytes 1638416 | tf_op jit(solution)/shard_map/all_gather | solution.py:151
  329.3 73.5 %reduce-scatter.5.cloned.1.call-done = f32[128,800]{0,1:T(8,128)} async-done(((f32[1024,800]{0,1:T(8,128)}), f32[128,800]{0,1:T(8,128)}) %reduce-scatter.5.cloned.1.call-update) | async-done | bytes 409616 | tf_op jit(solution)/shard_map/reduce_scatter | solution.py:163
  405.9 40.2 %all-reduce.8 = (f32[800]{0:T(1024)}, f32[800]{0:T(1024)}) all-reduce(f32[800]{0:T(1024)} %get-tuple-element.99, f32[800]{0:T(1024)} %get-tuple-element.98), channel_id=1, replica_groups=mesh['gene'=8,'cell'=4] {'gene','cell'}, use_global_device_ids=true, to_apply=%region_24.0 | all-reduce | flops 1600 | bytes 12800 | tf_op jit(solution)/shard_map/psum | solution.py:52
  451.2 40.1 %all-reduce.7 = (f32[800]{0:T(1024)}, f32[800]{0:T(1024)S(1)}) all-reduce(f32[800]{0:T(1024)} %get-tuple-element.97, f32[800]{0:T(1024)} %get-tuple-element.96), channel_id=1, replica_groups=mesh['gene'=8,'cell'=4] {'gene','cell'}, use_global_device_ids=true, to_apply=%region_28.0 | all-reduce | flops 1600 | bytes 12800 | tf_op jit(solution)/shard_map/psum | solution.py:52
  500.7 40.8 %all-reduce.6 = (f32[800]{0:T(1024)S(1)}, f32[800]{0:T(1024)S(1)}) all-reduce(f32[800]{0:T(1024)S(1)} %get-tuple-element.95, f32[800]{0:T(1024)S(1)} %get-tuple-element.94), channel_id=1, replica_groups=mesh['gene'=8,'cell'=4] {'gene','cell'}, use_global_device_ids=true, to_apply=%region_32.0 | all-reduce | flops 1600 | bytes 12800 | tf_op jit(solution)/shard_map/psum | solution.py:52
  544.5 39.6 %all-reduce.5 = (f32[]{:T(128)}, f32[800]{0:T(1024)S(1)}, f32[800]{0:T(1024)S(1)}, f32[2,100]{1,0:T(2,128)}) all-reduce(f32[]{:T(128)S(6)} %add.508, f32[800]{0:T(1024)S(1)} %get-tuple-element.93, f32[800]{0:T(1024)S(1)} %get-tuple-element.92, f32[2,100]{1,0:T(2,128)S(1)} %pad_maximum_fusion.7), channel_id=1, replica_groups=mesh['gene'=8,'cell'=4] {'gene','cell'}, use_global_device_ids=true, to_apply=%region_19.0 | all-reduce | flops 1801 | bytes 14408 | tf_op jit(solution)/shard_map/psum | solution.py:200
  589.9 43.0 %all-gather.10.cloned.1.call-done = bf16[1024,800]{0,1:T(8,128)(2,1)} async-done(((bf16[128,800]{0,1:T(8,128)(2,1)}), bf16[1024,800]{0,1:T(8,128)(2,1)}) %all-gather.10.cloned.1.call-update) | async-done | bytes 1638416 | tf_op jit(solution)/shard_map/all_gather | solution.py:189
  643.3 34.6 %all-reduce.36.cloned.1.call-done = (f32[800,224]{0,1:T(8,128)}, f32[224,800]{1,0:T(8,128)}) async-done(((f32[800,224]{0,1:T(8,128)}, f32[224,800]{1,0:T(8,128)}), (f32[800,224]{0,1:T(8,128)}, f32[224,800]{1,0:T(8,128)})) %all-reduce.36.cloned.1.call-update) | async-done | bytes 1433616 | tf_op jit(solution)/shard_map/psum | solution.py:196
  680.8 22.4 all-reduce.14
  710.7 7.0 copy.58
  719.6 192.5 %all-reduce.24.cloned.1.call-done = f32[2,800,800]{2,0,1:T(2,128)} async-done(((f32[2,800,800]{2,0,1:T(2,128)}), f32[2,800,800]{2,0,1:T(2,128)}) %all-reduce.24.cloned.1.call-update) | async-done | bytes 5120016
  914.4 92.0 %all-gather.12.cloned.1.call-done = f32[2,800,800]{2,0,1:T(2,128)} async-done(((f32[2,100,800]{2,0,1:T(2,128)}), f32[2,800,800]{2,0,1:T(2,128)}) %all-gather.12.cloned.1.call-update) | async-done | bytes 5120016 | tf_op jit(solution)/shard_map/all_gather | solution.py:228
  1006.4 32.3 %multiply_add_fusion.4 = f32[2,800,800]{2,1,0:T(8,128)S(1)} fusion(f32[2,800,800]{2,0,1:T(2,128)} %all-gather.12.cloned.1.call-done), kind=kOutput, calls=%fused_computation.9 | convolution fusion | flops 12291840000 | bytes 10240000 | tf_op jit(solution)/shard_map/bij,bjk->bik/dot_general | solution.py:229
  1052.0 7.0 copy.62
  1059.0 195.9 %all-reduce.26.cloned.1.call-done = f32[2,800,800]{2,0,1:T(2,128)} async-done(((f32[2,800,800]{2,0,1:T(2,128)}), f32[2,800,800]{2,0,1:T(2,128)}) %all-reduce.26.cloned.1.call-update) | async-done | bytes 5120016
  1257.0 91.9 %all-gather.14.cloned.1.call-done = f32[2,800,800]{2,0,1:T(2,128)} async-done(((f32[2,100,800]{2,0,1:T(2,128)}), f32[2,800,800]{2,0,1:T(2,128)}) %all-gather.14.cloned.1.call-update) | async-done | bytes 5120016 | tf_op jit(solution)/shard_map/all_gather | solution.py:228
  1348.9 32.2 %multiply_add_fusion.3 = f32[2,800,800]{2,1,0:T(8,128)S(1)} fusion(f32[2,800,800]{2,0,1:T(2,128)} %all-gather.14.cloned.1.call-done), kind=kOutput, calls=%fused_computation.8 | convolution fusion | flops 12291840000 | bytes 10240000 | tf_op jit(solution)/shard_map/bij,bjk->bik/dot_general | solution.py:229
  1394.3 7.0 copy.66
  1401.4 196.1 %all-reduce.28.cloned.1.call-done = f32[2,800,800]{2,0,1:T(2,128)} async-done(((f32[2,800,800]{2,0,1:T(2,128)}), f32[2,800,800]{2,0,1:T(2,128)}) %all-reduce.28.cloned.1.call-update) | async-done | bytes 5120016
  1627.4 64.4 %all-gather.16.cloned.1.call-done = f32[2,800,800]{2,0,1:T(2,128)} async-done(((f32[2,100,800]{2,0,1:T(2,128)}), f32[2,800,800]{2,0,1:T(2,128)}) %all-gather.16.cloned.1.call-update) | async-done | bytes 5120016 | tf_op jit(solution)/shard_map/all_gather | solution.py:228
  1691.8 31.6 %multiply_add_fusion.2 = f32[2,800,800]{2,1,0:T(8,128)S(1)} fusion(f32[2,800,800]{2,0,1:T(2,128)} %all-gather.16.cloned.1.call-done), kind=kOutput, calls=%fused_computation.7 | convolution fusion | flops 12291840000 | bytes 10240000 | tf_op jit(solution)/shard_map/bij,bjk->bik/dot_general | solution.py:229
  1737.7 7.0 copy.70
  1744.7 117.6 %all-reduce.34.cloned.1.call-done = (f32[800,800]{1,0:T(8,128)}, f32[2,800,100]{1,2,0:T(8,128)}, f32[100,800]{1,0:T(8,128)}, f32[800,800]{1,0:T(8,128)}) async-done(((f32[800,800]{1,0:T(8,128)}, f32[2,800,100]{1,2,0:T(8,128)}, f32[100,800]{1,0:T(8,128)}, f32[800,800]{1,0:T(8,128)}), (f32[800,800]{1,0:T(8,128)}, f32[2,800,100]{1,2,0:T(8,128)}, f32[100,800]{1,0:T(8,128)}, ...) | async-done | bytes 6080016 | tf_op jit(solution)/shard_map/psum | solution.py:200
  1878.4 185.1 %all-reduce.30.cloned.1.call-done = f32[2,800,800]{2,0,1:T(2,128)} async-done(((f32[2,800,800]{2,0,1:T(2,128)}), f32[2,800,800]{2,0,1:T(2,128)}) %all-reduce.30.cloned.1.call-update) | async-done | bytes 5120016
  2081.9 11.8 fusion.132
  2093.8 11.0 fusion.243
  2104.8 11.0 multiply_add_fusion.13
  2115.8 11.3 fusion.244
  2127.1 12.2 fusion.245
  2139.3 18.3 all-gather.18.cloned.1.call-done
  2157.6 32.3 %multiply_add_fusion.1 = f32[2,800,800]{2,1,0:T(8,128)S(1)} fusion(f32[2,800,800]{2,0,1:T(2,128)} %all-gather.18.cloned.1.call-done), kind=kOutput, calls=%fused_computation.6 | convolution fusion | flops 12291840000 | bytes 10240000 | tf_op jit(solution)/shard_map/bij,bjk->bik/dot_general | solution.py:229
  2203.1 7.0 copy.74
  2210.1 14.0 multiply_add_fusion.12
  2224.2 11.7 fusion.246
  2235.9 10.7 fusion.247
  2246.6 11.0 multiply_add_fusion.11
  2257.6 12.1 fusion.248
  2269.8 10.7 fusion.249
  2280.5 11.0 multiply_add_fusion.10
  2291.5 11.5 fusion.250
  2303.0 11.9 fusion.251
  2315.0 12.3 fusion.133
  2327.3 79.0 %all-reduce.32.cloned.1.call-done = f32[2,800,800]{2,0,1:T(2,128)} async-done(((f32[2,800,800]{2,0,1:T(2,128)}), f32[2,800,800]{2,0,1:T(2,128)}) %all-reduce.32.cloned.1.call-update) | async-done | bytes 5120016
  2413.4 10.6 fusion.265
  2424.0 11.2 multiply_add_fusion.8
  2435.2 11.9 fusion.266
  2447.1 10.8 fusion.267
  2457.9 11.2 multiply_add_fusion.7
  2469.1 11.9 fusion.268
  2481.0 10.8 fusion.269
  2491.8 11.3 multiply_add_fusion.6
  2503.0 11.8 fusion.270
  2514.9 10.7 fusion.271
  2525.7 11.1 multiply_add_fusion.5
  2536.7 12.1 fusion.272
  2548.9 10.8 fusion.273
  2559.7 12.4 multiply_subtract_fusion.1
  2572.1 12.6 multiply_subtract_fusion
  2585.8 32.3 %multiply_add_fusion = f32[2,800,800]{2,1,0:T(8,128)S(1)} fusion(f32[2,800,800]{2,0,1:T(2,128)} %all-gather.20.cloned.1.call-done), kind=kOutput, calls=%fused_computation.5 | convolution fusion | flops 12291840000 | bytes 10240000 | tf_op jit(solution)/shard_map/bij,bjk->bik/dot_general | solution.py:229
  (410 shorter events, 218.2 us)
Async XLA Ops:
  7.2 83.7 %reduce-scatter.3.cloned.1.call-start = ((), (), s32[]{:S(2)}) async-start(), calls=%async_computation.2 | async-start | bytes 3686400 | tf_op jit(solution)/shard_map/reduce_scatter | solution.py:126
  10.8 121.8 %copy-start = (f32[800,800]{1,0:T(8,128)S(1)}, f32[800,800]{1,0:T(8,128)}, u32[]{:S(2)}) copy-start(f32[800,800]{1,0:T(8,128)} %param.29) | copy-start | bytes 7680004
  10.9 309.5 %all-gather.8.cloned.1.call-start = ((), (), s32[]{:S(2)}) async-start(), calls=%async_computation.3 | async-start | bytes 1843200 | tf_op jit(solution)/shard_map/all_gather | solution.py:151
  13.6 161.0 %copy-start.62 = (f32[800]{0:T(1024)}, f32[800]{0:T(1024)S(1)}, u32[]{:S(2)}) copy-start(f32[800]{0:T(1024)S(1)} %get-tuple-element.114) | copy-start | bytes 9604
  13.6 161.6 %copy-start.68 = (f32[800]{0:T(1024)}, f32[800]{0:T(1024)S(1)}, u32[]{:S(2)}) copy-start(f32[800]{0:T(1024)S(1)} %get-tuple-element.113) | copy-start | bytes 9604
  13.6 162.2 %copy-start.72 = (f32[800]{0:T(1024)}, f32[800]{0:T(1024)S(1)}, u32[]{:S(2)}) copy-start(f32[800]{0:T(1024)S(1)} %get-tuple-element.112) | copy-start | bytes 9604
  13.6 162.2 %copy-start.89 = (f32[800]{0:T(1024)}, f32[800]{0:T(1024)S(1)}, u32[]{:S(2)}) copy-start(f32[800]{0:T(1024)S(1)} %get-tuple-element.111) | copy-start | bytes 9604
  13.7 211.2 %copy-start.64 = (f32[800]{0:T(1024)}, f32[800]{0:T(1024)S(1)}, u32[]{:S(2)}) copy-start(f32[800]{0:T(1024)S(1)} %get-tuple-element.110) | copy-start | bytes 9604
  132.6 43.2 %copy-start.73 = (f32[800]{0:T(1024)}, f32[800]{0:T(1024)S(1)}, u32[]{:S(2)}) copy-start(f32[800]{0:T(1024)S(1)} %get-tuple-element.160) | copy-start | bytes 9604
  135.1 44.3 %copy-start.22 = (f32[128,800]{0,1:T(8,128)}, f32[128,800]{0,1:T(8,128)S(1)}, u32[]{:S(2)}) copy-start(f32[128,800]{0,1:T(8,128)S(1)} %get-tuple-element.183) | copy-start | bytes 1228804
  175.3 47.6 %copy-start.60 = (f32[800]{0:T(1024)}, f32[800]{0:T(1024)S(1)}, u32[]{:S(2)}) copy-start(f32[800]{0:T(1024)S(1)} %get-tuple-element.179) | copy-start | bytes 9604
  182.1 264.7 %copy-start.16 = (f32[128,800]{0,1:T(8,128)}, f32[128,800]{0,1:T(8,128)S(1)}, u32[]{:S(2)}) copy-start(f32[128,800]{0,1:T(8,128)S(1)} %get-tuple-element.185) | copy-start | bytes 1228804
  274.0 128.8 %reduce-scatter.5.cloned.1.call-start = ((), (), s32[]{:S(2)}) async-start(), calls=%async_computation.4 | async-start | bytes 3686400 | tf_op jit(solution)/shard_map/reduce_scatter | solution.py:163
  328.0 304.9 %all-gather.10.cloned.1.call-start = ((), (), s32[]{:S(2)}) async-start(), calls=%async_computation.5 | async-start | bytes 1843200 | tf_op jit(solution)/shard_map/all_gather | solution.py:189
  491.9 49.6 %copy-start.15 = (f32[128,800]{0,1:T(8,128)S(1)}, f32[128,800]{0,1:T(8,128)}, u32[]{:S(2)}) copy-start(f32[128,800]{0,1:T(8,128)} %reduce-scatter.3.cloned.1.call-done) | copy-start | bytes 1228804
  496.2 45.3 %copy-start.105 = (f32[100]{0:T(128)S(1)}, f32[100]{0:T(128)}, u32[]{:S(2)}) copy-start(f32[100]{0:T(128)} %get-tuple-element.163) | copy-start | bytes 1204
  496.2 45.3 %copy-start.106 = (f32[100]{0:T(128)S(1)}, f32[100]{0:T(128)}, u32[]{:S(2)}) copy-start(f32[100]{0:T(128)} %get-tuple-element.175) | copy-start | bytes 1204
  500.7 83.5 %copy-start.88 = (f32[800]{0:T(1024)S(1)}, f32[800]{0:T(1024)}, u32[]{:S(2)}) copy-start(f32[800]{0:T(1024)} %get-tuple-element.159) | copy-start | bytes 9604
  541.5 42.7 %copy-start.91 = (f32[800]{0:T(1024)}, f32[800]{0:T(1024)S(1)}, u32[]{:S(2)}) copy-start(f32[800]{0:T(1024)S(1)} %get-tuple-element.121) | copy-start | bytes 9604
  541.5 45.0 %copy-start.84 = (f32[800]{0:T(1024)}, f32[800]{0:T(1024)S(1)}, u32[]{:S(2)}) copy-start(f32[800]{0:T(1024)S(1)} %get-tuple-element.120) | copy-start | bytes 9604
  541.5 45.0 %copy-start.81 = (f32[800]{0:T(1024)}, f32[800]{0:T(1024)S(1)}, u32[]{:S(2)}) copy-start(f32[800]{0:T(1024)S(1)} %broadcast_multiply_fusion.1) | copy-start | bytes 9604
  544.5 88.3 %copy-start.25 = (bf16[1024,224]{0,1:T(8,128)(2,1)S(1)}, bf16[1024,224]{0,1:T(8,128)(2,1)}, u32[]{:S(2)}) copy-start(bf16[1024,224]{0,1:T(8,128)(2,1)} %param.24) | copy-start | bytes 1376260
  584.1 51.8 %copy-start.87 = (f32[800]{0:T(1024)}, f32[800]{0:T(1024)S(1)}, u32[]{:S(2)}) copy-start(f32[800]{0:T(1024)S(1)} %get-tuple-element.117) | copy-start | bytes 9604
  584.1 51.8 %copy-start.92 = (f32[800]{0:T(1024)}, f32[800]{0:T(1024)S(1)}, u32[]{:S(2)}) copy-start(f32[800]{0:T(1024)S(1)} %get-tuple-element.118) | copy-start | bytes 9604
  586.5 91.4 %all-reduce.36.cloned.1.call-start = ((), (), s32[]{:S(2)}) async-start(), calls=%async_computation.17 | async-start | bytes 3211264 | tf_op jit(solution)/shard_map/psum | solution.py:196
  589.9 46.1 %copy-start.100 = (f32[224]{0:T(256)S(1)}, f32[224]{0:T(256)}, u32[]{:S(2)}) copy-start(f32[224]{0:T(256)} %get-tuple-element.88) | copy-start | bytes 2692
  589.9 52.3 %copy-start.107 = (f32[224]{0:T(256)S(1)}, f32[224]{0:T(256)}, u32[]{:S(2)}) copy-start(f32[224]{0:T(256)} %param.47) | copy-start | bytes 2692
  589.9 88.0 %copy-start.43 = (f32[800,224]{0,1:T(8,128)S(1)}, f32[800,224]{0,1:T(8,128)}, u32[]{:S(2)}) copy-start(f32[800,224]{0,1:T(8,128)} %param.44) | copy-start | bytes 2150404
  589.9 90.1 %copy-start.44 = (f32[224,800]{1,0:T(8,128)S(1)}, f32[224,800]{1,0:T(8,128)}, u32[]{:S(2)}) copy-start(f32[224,800]{1,0:T(8,128)} %param.39) | copy-start | bytes 2150404
  635.9 276.2 %all-reduce.24.cloned.1.call-start = ((), (), s32[]{:S(2)}) async-start(), calls=%async_computation.11 | async-start | bytes 11468800
  679.9 358.7 %copy-start.28 = (f32[800,224]{0,1:T(8,128)}, f32[800,224]{0,1:T(8,128)S(1)}, u32[]{:S(2)}) copy-start(f32[800,224]{0,1:T(8,128)S(1)} %get-tuple-element.158) | copy-start | bytes 2150404
  680.8 29.6 %copy-start.29 = (f32[224,800]{1,0:T(8,128)}, f32[224,800]{1,0:T(8,128)S(1)}, u32[]{:S(2)}) copy-start(f32[224,800]{1,0:T(8,128)S(1)} %get-tuple-element.156) | copy-start | bytes 2150404
  717.7 288.7 %all-gather.12.cloned.1.call-start = ((), (), s32[]{:S(2)}) async-start(), calls=%async_computation.6 | async-start | bytes 6451200 | tf_op jit(solution)/shard_map/all_gather | solution.py:228
  914.2 340.6 %all-reduce.26.cloned.1.call-start = ((), (), s32[]{:S(2)}) async-start(), calls=%async_computation.12 | async-start | bytes 11468800
  1058.9 290.0 %all-gather.14.cloned.1.call-start = ((), (), s32[]{:S(2)}) async-start(), calls=%async_computation.7 | async-start | bytes 6451200 | tf_op jit(solution)/shard_map/all_gather | solution.py:228
  1257.0 340.6 %all-reduce.28.cloned.1.call-start = ((), (), s32[]{:S(2)}) async-start(), calls=%async_computation.13 | async-start | bytes 11468800
  1401.3 200.6 %copy-start.74 = (f32[800]{0:T(1024)S(1)}, f32[800]{0:T(1024)}, u32[]{:S(2)}) copy-start(f32[800]{0:T(1024)} %copy-done.73) | copy-start | bytes 9604
  1401.3 200.6 %copy-start.76 = (f32[800]{0:T(1024)S(1)}, f32[800]{0:T(1024)}, u32[]{:S(2)}) copy-start(f32[800]{0:T(1024)} %copy-done.75) | copy-start | bytes 9604
  1401.3 200.6 %copy-start.61 = (f32[800]{0:T(1024)S(1)}, f32[800]{0:T(1024)}, u32[]{:S(2)}) copy-start(f32[800]{0:T(1024)} %copy-done.60) | copy-start | bytes 9604
  1401.3 200.6 %copy-start.78 = (f32[800]{0:T(1024)S(1)}, f32[800]{0:T(1024)}, u32[]{:S(2)}) copy-start(f32[800]{0:T(1024)} %copy-done.77) | copy-start | bytes 9604
  1401.3 213.4 %copy-start.53 = (bf16[128,100]{0,1:T(8,128)(2,1)S(1)}, bf16[128,100]{0,1:T(8,128)(2,1)}, u32[]{:S(2)}) copy-start(bf16[128,100]{0,1:T(8,128)(2,1)} %copy-done.52) | copy-start | bytes 76804
  1401.3 290.5 %all-gather.16.cloned.1.call-start = ((), (), s32[]{:S(2)}) async-start(), calls=%async_computation.8 | async-start | bytes 6451200 | tf_op jit(solution)/shard_map/all_gather | solution.py:228
  1599.6 17.3 copy-start.51
  1599.6 18.3 copy-start.17
  1599.6 18.3 copy-start.18
  1599.6 18.3 copy-start.26
  1599.6 18.3 copy-start.59
  1599.6 18.3 copy-start.65
  1599.6 18.3 copy-start.70
  1599.7 262.6 %all-reduce.34.cloned.1.call-start = ((), (), s32[]{:S(2)}) async-start(), calls=%async_computation.16 | async-start | bytes 13705216 | tf_op jit(solution)/shard_map/psum | solution.py:200
  1599.7 17.2 copy-start.41
  1624.7 438.8 %all-reduce.30.cloned.1.call-start = ((), (), s32[]{:S(2)}) async-start(), calls=%async_computation.14 | async-start | bytes 11468800
  1626.1 97.4 %copy-start.56 = (f32[2,4,800]{2,1,0:T(4,128)}, f32[2,4,800]{2,1,0:T(4,128)S(1)}, u32[]{:S(2)}) copy-start(f32[2,4,800]{2,1,0:T(4,128)S(1)} %get-tuple-element.146) | copy-start | bytes 76804
  1744.6 117.7 %copy-start.46 = (f32[2,800,100]{1,0,2:T(2,128)S(1)}, f32[2,800,100]{1,0,2:T(2,128)}, u32[]{:S(2)}) copy-start(f32[2,800,100]{1,0,2:T(2,128)} %param.41) | copy-start | bytes 1920004
  1744.6 413.0 %all-gather.18.cloned.1.call-start = ((), (), s32[]{:S(2)}) async-start(), calls=%async_computation.9 | async-start | bytes 6451200 | tf_op jit(solution)/shard_map/all_gather | solution.py:228
  1873.9 202.9 %copy-start.48 = (f32[100,800]{1,0:T(8,128)}, f32[100,800]{1,0:T(8,128)S(1)}, u32[]{:S(2)}) copy-start(f32[100,800]{1,0:T(8,128)S(1)} %get-tuple-element.150) | copy-start | bytes 960004
  1878.4 190.9 %copy-start.31 = (f32[2,800,100]{1,2,0:T(8,128)S(1)}, f32[2,800,100]{1,2,0:T(8,128)}, u32[]{:S(2)}) copy-start(f32[2,800,100]{1,2,0:T(8,128)} %copy.57) | copy-start | bytes 1920004
  2065.5 340.8 %all-reduce.32.cloned.1.call-start = ((), (), s32[]{:S(2)}) async-start(), calls=%async_computation.15 | async-start | bytes 11468800
  2157.6 32.3 %copy-start.10 = (f32[800,224]{0,1:T(8,128)S(1)}, f32[800,224]{0,1:T(8,128)}, u32[]{:S(2)}) copy-start(f32[800,224]{0,1:T(8,128)} %copy-done.9) | copy-start | bytes 2150404
  2210.1 375.7 %all-gather.20.cloned.1.call-start = ((), (), s32[]{:S(2)}) async-start(), calls=%async_computation.10 | async-start | bytes 6451200 | tf_op jit(solution)/shard_map/all_gather | solution.py:228
  2572.1 13.2 copy-start.99
  2572.1 13.2 copy-start.101
  2585.8 32.4 %copy-start.4 = (f32[800,224]{0,1:T(8,128)S(1)}, f32[800,224]{0,1:T(8,128)}, u32[]{:S(2)}) copy-start(f32[800,224]{0,1:T(8,128)} %copy-done.3) | copy-start | bytes 2150404
  2585.8 32.4 %copy-start.21 = (f32[800,224]{0,1:T(8,128)S(1)}, f32[800,224]{0,1:T(8,128)}, u32[]{:S(2)}) copy-start(f32[800,224]{0,1:T(8,128)} %param.33) | copy-start | bytes 2150404
  (61 other events, 261.9 us)
Sparse Core Ops, SparseCore 0:
  11.6 79.1 reduce-scatter.2
  274.1 46.2 all-gather.7
  328.1 74.7 reduce-scatter.4
  586.6 46.1 all-gather.9
  636.1 41.7 all-reduce.35
  717.8 194.2 all-reduce.23
  915.1 91.2 all-gather.11
  1059.1 195.7 all-reduce.25
  1257.6 91.2 all-gather.13
  1401.4 196.0 all-reduce.27
  1600.5 91.2 all-gather.15
  1700.3 161.9 all-reduce.33
  1866.0 197.4 all-reduce.29
  2066.3 91.3 all-gather.17
  2210.2 196.0 all-reduce.31
  2408.5 91.2 all-gather.19
where the time goes:
time: 2650 us; the launch traced here: 2630 us
  waiting for transfers between devices  1510 us (57%)
  matrix products  645 us (24%)
  blocking collectives  350 us (13%)
  local copies, waits for them, and re-layouts  70.2 us (3%)
  other arithmetic  36.4 us (1%)
    unnamed x21, waiting for transfers between devices  849 us
    dot_general x95, matrix products, matmul(): jnp.dot(left, right, precision=HIGH, preferred_element_type=jnp.float32)  433 us
    all_gather x5, waiting for transfers between devices, shards(): whole = lax.all_gather(shares, 'gene', axis=1, tiled=True)  267 us
    dot_general x5, matrix products, shards(): jnp.einsum('bij,bjk->bik', whole, whole, precision=HIGH)  161 us
    psum x4, blocking collectives, normalize(): lax.psum((jnp.sum(values, axis=0), jnp.sum(values * values, axis=0)), ('g...  160 us
    psum x3, blocking collectives, norm_back(): lax.psum((jnp.sum(grad_shift, axis=0), jnp.sum(grad_shift * scaled, axis=...  121 us
    psum x1, waiting for transfers between devices, shards(): lax.psum((grad_enc_mid, grad_latent_w, grad_dec_in, decoder_middle_gradie...  118 us
    reduce_scatter x1, waiting for transfers between devices, shards(): lax.psum_scatter(jnp.dot(block, encoder_input_reduced, preferred_element_...  76.7 us
  transfers between devices with their start and end apart: 16, of which 15 were waited for; matrix products, arithmetic and copies ran while one was open for 18% of the time, Pallas kernels for 0%

commit v1 on v0

v1 whole, which is shorter than its diff:
```python
import math

import jax
import jax.numpy as jnp
from jax import lax
from jax.experimental import pallas as pl
from jax.experimental.pallas import tpu as pltpu
from jax.sharding import PartitionSpec as P

NS = 5


EPSILON = 1e-05
ALPHA_KL = 5e-05
MOMENTUM = 0.95
RATE = 0.5
RATE_VECTOR = 0.2
COEF_A = 3.4445
COEF_B = -4.775
COEF_C = 2.0315


def inner_rows(left, right):
    return lax.dot_general(
        left, right, (((0,), (0,)), ((), ())), preferred_element_type=jnp.float32
    )


def outer_cols(left, right):
    return lax.dot_general(
        left, right, (((1,), (1,)), ((), ())), preferred_element_type=jnp.float32
    )


def rows_times(left, right):
    return jnp.dot(left, right, preferred_element_type=jnp.float32)


def low(values):
    return values.astype(jnp.bfloat16)


def pair_tree(values):
    while len(values) > 1:
        values = [values[at] + values[at + 1] for at in range(0, len(values), 2)]
    return values[0]


def swap(values, distance, axis):
    pairs = [(device, device ^ distance) for device in range(lax.axis_size(axis))]
    return lax.ppermute(values, axis, pairs)


def cell_sum(values):
    count = lax.axis_size("cell")
    if count & (count - 1):
        return lax.psum(values, "cell")
    return pair_tree(
        [values] + [swap(values, distance, "cell") for distance in range(1, count)]
    )


def cell_scatter(blocks):
    count = lax.axis_size("cell")
    me = lax.axis_index("cell")

    def block(owner):
        return lax.dynamic_index_in_dim(blocks, owner, 0, keepdims=False)

    return pair_tree(
        [block(me)]
        + [swap(block(me ^ distance), distance, "cell") for distance in range(1, count)]
    )


def gene_gather(values):
    count = lax.axis_size("gene")
    me = lax.axis_index("gene")
    gathered = jnp.zeros((count,) + values.shape, values.dtype)
    for distance in range(0, count, 2):
        near = values if distance == 0 else swap(values, distance, "gene")
        far = swap(near, 1, "gene")
        gathered = lax.dynamic_update_index_in_dim(gathered, near, me ^ distance, 0)
        gathered = lax.dynamic_update_index_in_dim(gathered, far, me ^ distance ^ 1, 0)
    return gathered.reshape((count * values.shape[0],) + values.shape[1:])


def scatter_pieces(pieces, moments):
    count = lax.axis_size("cell")
    width = pieces[0].shape[1]

    def pack(entries):
        blocks = [entry.reshape(count, -1, width) for entry in entries]
        rows = sum(block.shape[1] for block in blocks)
        blocks.append(jnp.zeros((count, -rows % 8, width), jnp.float32))
        return jnp.concatenate(blocks, axis=1)

    known = [
        jnp.zeros_like(piece) if moment is None else MOMENTUM * moment
        for piece, moment in zip(pieces, moments)
    ]
    known = lax.dynamic_index_in_dim(pack(known), lax.axis_index("cell"), 0, keepdims=False)
    return cell_scatter(pack(pieces)) + known


def join(values, distance, axis, at):
    other = swap(values, distance, axis)
    upper = (lax.axis_index(axis) & distance) != 0
    return jnp.stack(
        [jnp.where(upper, other, values), jnp.where(upper, values, other)], axis=at
    )


def spread(values, axis, at=0):
    shape = values.shape
    distance = lax.axis_size(axis) // 2
    place = at
    while distance:
        values = join(values, distance, axis, place)
        distance //= 2
        place += 1
    return values.reshape(shape[:at] + (lax.axis_size(axis),) + shape[at:])


def cell_total(values, kind=jnp.float32):
    count = lax.axis_size("cell")
    me = lax.axis_index("cell")
    distance = 1
    while distance < count:
        half = values.shape[0] // 2
        upper = ((me & distance) != 0).astype(jnp.int32)
        keep = lax.dynamic_slice_in_dim(values, upper * half, half, 0)
        give = lax.dynamic_slice_in_dim(values, (1 - upper) * half, half, 0)
        values = keep + swap(give, distance, "cell")
        distance *= 2
    if kind == jnp.bfloat16:
        values = low(lax.reduce_precision(values, 8, 7))
    while distance > 1:
        distance //= 2
        values = join(values, distance, "cell", 0).reshape(-1, values.shape[1])
    return values.astype(jnp.float32)


def by_core(mine):
    other = swap(mine, 1, "cell")
    odd = (lax.axis_index("cell") & 1) != 0
    return jnp.where(odd, other, mine), jnp.where(odd, mine, other)


def gather_pieces(block, heights):
    count = lax.axis_size("cell")
    gathered = lax.all_gather(block, ("gene", "cell"), axis=0, tiled=False)
    start = 0
    whole = []
    for height in heights:
        part = gathered[:, start : start + height // count]
        whole.append(part.reshape(-1, part.shape[2]))
        start += height // count
    return whole


def gather_slices(pieces, moments):
    slices = [
        cell_sum(piece) if moment is None else cell_sum(piece) + MOMENTUM * moment
        for piece, moment in zip(pieces, moments)
    ]
    return slices[:1] + [gather_rows(values, "gene") for values in slices[1:]]


def lengthen(values, axis, multiple):
    room = [(0, 0)] * values.ndim
    room[axis] = (0, -values.shape[axis] % multiple)
    return jnp.pad(values, room)


def three_parts(values):
    first = lax.reduce_precision(values, 8, 7)
    second = lax.reduce_precision(values - first, 8, 7)
    return low(jnp.stack([first, second, values - first - second], axis=1))


def gather_rows(values, axes):
    return lax.all_gather(values, axes, axis=0, tiled=True)


def rescale(values, batch_mean, inverse, norm_params, layer):
    scaled = (values - batch_mean) * inverse
    return scaled, scaled * norm_params[0, layer] + norm_params[1, layer]


def normalize(values, norm_params, layer, cells):
    totals = cell_sum(jnp.stack([jnp.sum(values, axis=0), jnp.sum(values * values, axis=0)]))
    batch_mean = totals[0] / cells
    batch_var = totals[1] / cells - batch_mean * batch_mean
    inverse = lax.rsqrt(batch_var + EPSILON)
    scaled, shifted = rescale(values, batch_mean, inverse, norm_params, layer)
    return (low(jax.nn.gelu(shifted)), (values, inverse, batch_mean, batch_var))


def norm_back(grad_out, saved, norm_params, layer, cells):
    values, inverse, batch_mean = lax.optimization_barrier(saved[:3])
    scaled, shifted = rescale(values, batch_mean, inverse, norm_params, layer)
    unused, pullback = jax.vjp(jax.nn.gelu, shifted)
    grad_shift = pullback(grad_out)[0]
    sums = cell_sum(jnp.stack([jnp.sum(grad_shift, axis=0), jnp.sum(grad_shift * scaled, axis=0)]))
    grad_in = (
        norm_params[0, layer] * inverse * (grad_shift - sums[0] / cells - scaled * sums[1] / cells)
    )
    return (low(grad_in), sums[1], sums[0])


def orthogonal_shared(own):
    total = lax.psum(jnp.sum(own * own), "gene")
    current = own / (jnp.sqrt(total) + 1e-07)
    for iteration in range(NS):
        operand = low(current)
        gram = lax.psum(inner_rows(operand, operand), "gene")
        gram_low = low(gram)
        polynom = low(COEF_B * gram + COEF_C * rows_times(gram_low, gram_low))
        current = COEF_A * current + rows_times(operand, polynom)
    return current


def iterate(operand, gram, gram_low, polynom, own=None, own_low=None):
    gram[...] = outer_cols(operand[...], operand[...])
    gram_low[...] = low(gram[...])
    square = rows_times(gram_low[...], gram_low[...])
    polynom[...] = low(COEF_B * gram[...] + COEF_C * square)
    if own is not None:
        own[...] = COEF_A * own[...] + rows_times(polynom[...], own_low[...])
        own_low[...] = low(own[...])


def square_kernel(place, even, odd, result, current, operand, gram, gram_low, polynom):
    def load(moment):
        values = moment[...]
        current[...] = values * (1.0 / (jnp.sqrt(jnp.sum(values * values)) + 1e-07))

    pl.when(place[0] == 0)(lambda: load(even))
    pl.when(place[0] != 0)(lambda: load(odd))

    def step(iteration, carry):
        operand[...] = low(current[...])
        iterate(operand, gram, gram_low, polynom)
        current[...] = COEF_A * current[...] + rows_times(polynom[...], operand[...])
        return carry

    lax.fori_loop(0, NS, step, 0)
    result[...] = low(current[...])


def tall_kernel(
    place, even, odd, result, current, operand, own, own_low, gram, gram_low, polynom
):
    rows = even.shape[0]
    tile = 256

    def load(moment):
        def add_square(at, total):
            values = moment[pl.ds(pl.multiple_of(at * tile, tile), tile), :].astype(jnp.float32)
            return total + jnp.sum(values * values)

        total = lax.fori_loop(0, rows // tile, add_square, jnp.float32(0))
        scale = 1.0 / (jnp.sqrt(total) + 1e-07)

        def turn(at, carry):
            here = pl.ds(pl.multiple_of(at * tile, tile), tile)
            values = moment[here, :].astype(jnp.float32).T * scale
            current[:, here] = values
            operand[:, here] = low(values)
            return carry

        lax.fori_loop(0, rows // tile, turn, 0)
        mine = pl.ds(pl.multiple_of(place[1], 16), own.shape[1])
        own[...] = moment[mine, :].astype(jnp.float32).T * scale
        own_low[...] = low(own[...])

    pl.when(place[0] == 0)(lambda: load(even))
    pl.when(place[0] != 0)(lambda: load(odd))

    def step(iteration, carry):
        iterate(operand, gram, gram_low, polynom, own, own_low)

        @pl.when(iteration < NS - 1)
        def _():
            current[...] = COEF_A * current[...] + rows_times(polynom[...], operand[...])
            operand[...] = low(current[...])

        return carry

    lax.fori_loop(0, NS, step, 0)
    result[...] = low(own[...].T)


def narrow_kernel(moments, results):
    for number in range(moments.shape[0]):
        values = moments[number]
        results[number] = values / (jnp.sqrt(jnp.sum(values * values)) + 1e-07)
    exact = dict(precision=lax.Precision.HIGHEST, preferred_element_type=jnp.float32)

    def step(iteration, carry):
        for number in range(moments.shape[0]):
            values = results[number]
            gram = lax.dot_general(values, values, (((1,), (1,)), ((), ())), **exact)
            polynom = COEF_B * gram + COEF_C * jnp.dot(gram, gram, **exact)
            results[number] = COEF_A * values + jnp.dot(polynom, values, **exact)
        return carry

    lax.fori_loop(0, NS, step, 0)


def on_chip(kernel, shape, scratch, flops, *operands):
    space = pl.BlockSpec(memory_space=pltpu.VMEM)
    scalars = pl.BlockSpec(memory_space=pltpu.SMEM)
    return pl.pallas_call(
        kernel,
        out_shape=shape,
        in_specs=[scalars if operand.dtype == jnp.int32 else space for operand in operands],
        out_specs=space,
        scratch_shapes=[pltpu.VMEM(*entry) for entry in scratch],
        compiler_params=pltpu.CompilerParams(vmem_limit_bytes=48 * 2**20),
        cost_estimate=pl.CostEstimate(flops=flops, bytes_accessed=2**22, transcendentals=0),
    )(*operands)


def pair_place():
    return (lax.axis_index("cell") & 1).astype(jnp.int32)


def orthogonal_squares(even, odd):
    width = even.shape[0]
    mine = on_chip(
        square_kernel,
        jax.ShapeDtypeStruct(even.shape, jnp.bfloat16),
        [
            ((width, width), jnp.float32),
            ((width, width), jnp.bfloat16),
            ((width, width), jnp.float32),
            ((width, width), jnp.bfloat16),
            ((width, width), jnp.bfloat16),
        ],
        6 * NS * width**3,
        pair_place()[None],
        even,
        odd,
    )
    return by_core(mine)


def orthogonal_talls(even, odd, own_rows):
    rows, width = even.shape
    start = (lax.axis_index("gene") * own_rows).astype(jnp.int32)
    mine = on_chip(
        tall_kernel,
        jax.ShapeDtypeStruct((own_rows, width), jnp.bfloat16),
        [
            ((width, rows), jnp.float32),
            ((width, rows), jnp.bfloat16),
            ((width, own_rows), jnp.float32),
            ((width, own_rows), jnp.bfloat16),
            ((width, width), jnp.float32),
            ((width, width), jnp.bfloat16),
            ((width, width), jnp.bfloat16),
        ],
        2 * NS * width * width * (2 * rows + width),
        jnp.stack([pair_place(), start]),
        even,
        odd,
    )
    return by_core(mine)


def orthogonal_narrow(moments):
    count, width, length = moments.shape
    return on_chip(
        narrow_kernel,
        jax.ShapeDtypeStruct(moments.shape, jnp.float32),
        [],
        12 * NS * count * width * width * (2 * length + width),
        moments,
    )


def vector_step(value, moment, square):
    return value - RATE_VECTOR * moment * lax.rsqrt(square + 1e-06)


def shards(
    counts,
    study,
    study_gene_mask,
    noise,
    enc_in,
    enc_mid,
    latent_w,
    dec_in,
    dec_mid,
    dec_out,
    norm_params,
    latent_bias,
    out_bias,
    running_mean,
    running_variance,
    mom_enc_in,
    mom_enc_mid,
    mom_latent_w,
    mom_dec_in,
    mom_dec_mid,
    mom_dec_out,
    mom_norm,
    mom_latent_bias,
    mom_out_bias,
):
    gene_count = lax.axis_size("gene")
    cell_count = lax.axis_size("cell")
    gene_at = lax.axis_index("gene")
    cell_at = lax.axis_index("cell")
    group_rows, gene_local = counts.shape
    cells = group_rows * cell_count
    genes = gene_local * gene_count
    hidden_width = enc_mid.shape[0]
    latent_width = dec_in.shape[0]
    study_labels = study_gene_mask.shape[0]
    devices = gene_count * cell_count
    whole = (
        group_rows * genes <= 2**22
        and genes * hidden_width <= 2**21
        and genes % 256 == 0
        and hidden_width % devices == 0
        and gene_local % (8 * cell_count) == 0
        and devices & (devices - 1) == 0
    )

    def own_rows(values, rows=gene_local):
        return lax.dynamic_slice_in_dim(values, gene_at * rows, rows, 0)

    selection = low(study[None, :] == jnp.arange(study_labels, dtype=jnp.int32)[:, None])
    enc_in_low = low(enc_in)
    enc_mid_low = low(enc_mid)
    latent_low = low(latent_w)
    dec_in_low = low(dec_in)
    dec_mid_low = low(dec_mid)
    dec_out_low = low(dec_out)
    counts_turned = counts.T
    last_layer = jnp.concatenate(
        [dec_out_low.T, low(study_gene_mask.T), three_parts(out_bias)], axis=1
    )
    if whole:
        part = gene_local // cell_count

        def own_part(values):
            return lax.dynamic_slice_in_dim(values, cell_at * part, part, 0)

        counts_turned = gene_gather(counts_turned)
        enc_in_low = spread(spread(own_part(enc_in_low), "gene"), "cell", 1)
        enc_in_low = enc_in_low.reshape(genes, hidden_width)
        first = inner_rows(counts_turned, enc_in_low)
        all_noise = spread(noise, "gene").reshape(group_rows, latent_width)
        last_layer = gather_rows(own_part(last_layer), ("gene", "cell"))
    else:
        first = lax.psum(inner_rows(counts_turned, enc_in_low), "gene")
        all_noise = gather_rows(noise, "gene")
    dec_out_turned = last_layer[:, :hidden_width]
    mask_turned = last_layer[:, hidden_width : hidden_width + study_labels]
    bias_column = jnp.sum(
        last_layer[:, hidden_width + study_labels :].astype(jnp.float32), axis=1, keepdims=True
    )
    one_low, saved_one = normalize(first, norm_params, 0, cells)
    second = rows_times(one_low, enc_mid_low)
    two_low, saved_two = normalize(second, norm_params, 1, cells)
    latent_mean = rows_times(two_low, latent_low[0]) + latent_bias[0]
    latent_logvar = rows_times(two_low, latent_low[1]) + latent_bias[1]
    spread_factor = jnp.exp(0.5 * latent_logvar)
    sample_low = low(latent_mean + all_noise * spread_factor)
    third = rows_times(sample_low, dec_in_low)
    three_low, saved_three = normalize(third, norm_params, 2, cells)
    fourth = rows_times(three_low, dec_mid_low)
    four_low, saved_four = normalize(fourth, norm_params, 3, cells)
    decoded = outer_cols(dec_out_turned, four_low) + bias_column
    error = decoded - counts_turned.astype(jnp.float32)
    gene_mask = rows_times(mask_turned, selection)
    loss_part = 0.5 / genes * jnp.sum(gene_mask * error * error)
    grad_decoded = low(gene_mask * error / genes)
    grad_four = inner_rows(grad_decoded, dec_out_turned)
    if whole:
        own_grad = own_rows(grad_decoded)
    else:
        loss_part, grad_four = lax.psum((loss_part, grad_four), "gene")
        own_grad = grad_decoded
    recon = low(rows_times(four_low, dec_out_low) + out_bias)
    kl_scale = ALPHA_KL / genes
    loss_part = loss_part + kl_scale * 0.5 * jnp.sum(
        jnp.exp(latent_logvar) + latent_mean * latent_mean - 1.0 - latent_logvar
    )
    grad_dec_out = rows_times(own_grad, four_low)
    grad_out_bias = jnp.sum(own_grad, axis=1, dtype=jnp.float32)

    def bias_rows(values):
        return lengthen(values.reshape(cell_count, -1), 1, hidden_width)

    pieces = [grad_dec_out, bias_rows(grad_out_bias)]
    moments = [mom_dec_out.T, bias_rows(mom_out_bias)]
    if whole:
        decoder = scatter_pieces(pieces, moments)
    else:
        own_moment_out, moment_bias = gather_slices(pieces, moments)
    grad_a4, gain_four, shift_four = norm_back(grad_four, saved_four, norm_params, 3, cells)
    grad_dec_mid = cell_total(inner_rows(three_low, grad_a4), jnp.bfloat16)
    grad_three = outer_cols(grad_a4, dec_mid_low)
    grad_a3, gain_three, shift_three = norm_back(grad_three, saved_three, norm_params, 2, cells)
    if whole:
        decoder, grad_a3 = lax.optimization_barrier((decoder, grad_a3))
        moment_out, moment_bias = gather_pieces(decoder, [gene_local, cell_count])
        own_moment_out = own_rows(moment_out)
    grad_dec_in = inner_rows(sample_low, grad_a3)
    grad_sample = outer_cols(grad_a3, dec_in_low)
    grad_mean = low(grad_sample + kl_scale * latent_mean)
    grad_logvar = low(
        grad_sample * all_noise * 0.5 * spread_factor
        + kl_scale * 0.5 * (jnp.exp(latent_logvar) - 1.0)
    )
    grad_pair = jnp.concatenate([grad_mean, grad_logvar], axis=1)
    latent_pair = jnp.concatenate([latent_low[0], latent_low[1]], axis=1)
    grad_narrow = jnp.concatenate([inner_rows(grad_pair, two_low), grad_dec_in])
    grad_narrow = cell_total(lengthen(grad_narrow, 0, 8 * cell_count))
    small = cell_sum(
        jnp.concatenate([jnp.sum(grad_pair, axis=0, dtype=jnp.float32), loss_part[None]])
    )
    grad_two = outer_cols(grad_pair, latent_pair)
    grad_a2, gain_two, shift_two = norm_back(grad_two, saved_two, norm_params, 1, cells)
    grad_enc_mid = cell_total(inner_rows(one_low, grad_a2), jnp.bfloat16)
    grad_one = outer_cols(grad_a2, enc_mid_low)
    grad_a1, gain_one, shift_one = norm_back(grad_one, saved_one, norm_params, 0, cells)
    grad_enc_in = inner_rows(counts, grad_a1)
    if whole:
        encoder = scatter_pieces([grad_enc_in], [mom_enc_in])
        moment_first = gather_pieces(low(encoder), [gene_local])[0]
        new_mom_enc_in = own_rows(moment_first).astype(jnp.float32)
    else:
        new_mom_enc_in = MOMENTUM * mom_enc_in + cell_sum(grad_enc_in)
    new_mom_dec_out = own_moment_out.T

    grad_latent_bias = small[: 2 * latent_width].reshape(2, latent_width)
    total = small[2 * latent_width]
    moment_bias = moment_bias[:, : gene_local // cell_count].reshape(gene_count, gene_local)
    new_mom_out_bias = lax.dynamic_index_in_dim(moment_bias, gene_at, 0, keepdims=False)
    new_out_bias = vector_step(out_bias, new_mom_out_bias, jnp.mean(moment_bias * moment_bias))

    new_mom_dec_mid = MOMENTUM * mom_dec_mid + grad_dec_mid
    new_mom_enc_mid = MOMENTUM * mom_enc_mid + grad_enc_mid
    turned_enc_mid, turned_dec_mid = orthogonal_squares(new_mom_enc_mid, new_mom_dec_mid)
    new_enc_mid = enc_mid - RATE * turned_enc_mid.astype(jnp.float32)
    new_dec_mid = dec_mid - RATE * turned_dec_mid.astype(jnp.float32)

    grad_latent = grad_narrow[: 2 * latent_width].reshape(2, latent_width, hidden_width)
    grad_dec_in = grad_narrow[2 * latent_width : 3 * latent_width]
    new_mom_dec_in = MOMENTUM * mom_dec_in + grad_dec_in
    turned_latent = MOMENTUM * jnp.swapaxes(mom_latent_w, 1, 2) + grad_latent
    new_mom_latent_w = jnp.swapaxes(turned_latent, 1, 2)
    narrow = orthogonal_narrow(jnp.concatenate([turned_latent, new_mom_dec_in[None]]))
    factor = math.sqrt(max(1.0, hidden_width / latent_width))
    new_dec_in = dec_in - RATE * factor * narrow[2]
    new_latent_w = latent_w - RATE * jnp.swapaxes(narrow[:2], 1, 2)

    if whole:
        turned_in, turned_out = orthogonal_talls(moment_first, moment_out, gene_local)
    else:
        turned_in = orthogonal_shared(new_mom_enc_in)
        turned_out = orthogonal_shared(own_moment_out)
    new_enc_in = enc_in - RATE * turned_in.astype(jnp.float32)
    factor = math.sqrt(max(1.0, genes / hidden_width))
    new_dec_out = dec_out - RATE * factor * turned_out.astype(jnp.float32).T

    grad_norm = jnp.stack(
        [
            jnp.stack([gain_one, gain_two, gain_three, gain_four]),
            jnp.stack([shift_one, shift_two, shift_three, shift_four]),
        ]
    )
    new_mom_norm = MOMENTUM * mom_norm + grad_norm
    new_norm = vector_step(
        norm_params, new_mom_norm, jnp.mean(new_mom_norm * new_mom_norm, axis=-1, keepdims=True)
    )
    new_mom_latent_bias = MOMENTUM * mom_latent_bias + grad_latent_bias
    new_latent_bias = vector_step(
        latent_bias,
        new_mom_latent_bias,
        jnp.mean(new_mom_latent_bias * new_mom_latent_bias, axis=-1, keepdims=True),
    )
    means = jnp.stack([saved_one[2], saved_two[2], saved_three[2], saved_four[2]])
    variances = jnp.stack([saved_one[3], saved_two[3], saved_three[3], saved_four[3]])
    new_running_mean = 0.9 * running_mean + 0.1 * means
    updated_running_variance = 0.9 * running_variance + 0.1 * variances * (cells / (cells - 1.0))
    return (
        recon,
        total / cells,
        new_enc_in,
        new_mom_enc_in,
        new_enc_mid,
        new_mom_enc_mid,
        new_latent_w,
        new_mom_latent_w,
        new_dec_in,
        new_mom_dec_in,
        new_dec_mid,
        new_mom_dec_mid,
        new_dec_out,
        new_mom_dec_out,
        new_norm,
        new_mom_norm,
        new_latent_bias,
        new_mom_latent_bias,
        new_out_bias,
        new_mom_out_bias,
        new_running_mean,
        updated_running_variance,
    )


def solution(mesh):
    in_specs = (
        P("cell", "gene"),
        P("cell"),
        P(None, "gene"),
        P(("cell", "gene"), None),
        P("gene", None),
        P(),
        P(),
        P(),
        P(),
        P(None, "gene"),
        P(),
        P(),
        P("gene"),
        P(),
        P(),
        P("gene", None),
        P(),
        P(),
        P(),
        P(),
        P(None, "gene"),
        P(),
        P(),
        P("gene"),
    )
    out_specs = (
        P("cell", "gene"),
        P(),
        P("gene", None),
        P("gene", None),
        P(),
        P(),
        P(),
        P(),
        P(),
        P(),
        P(),
        P(),
        P(None, "gene"),
        P(None, "gene"),
        P(),
        P(),
        P(),
        P(),
        P("gene"),
        P("gene"),
        P(),
        P(),
    )
    return jax.shard_map(shards, mesh=mesh, in_specs=in_specs, out_specs=out_specs, check_vma=False)
```

time: 2650 us -> 486 us (0.18)
  waiting for transfers between devices: 1510 us -> 146 us
  matrix products: 645 us -> 58.9 us
  blocking collectives: 350 us -> 0 us
  Pallas kernels: 0 us -> 104 us
  starting transfers between devices: 1.01 us -> 52.2 us
  local copies, waits for them, and re-layouts: 70.2 us -> 41.7 us
    unnamed x21 -> x3, waiting for transfers between devices: 849 us -> 0.05 us
    dot_general x108 -> x8, matrix products: 614 us -> 13.5 us  [rows_times(): return jnp.dot(left, right, preferred_element_type=jnp.float32)]
    all_gather x7 -> x3, waiting for transfers between devices: 356 us -> 0.02 us  [the longest x1 0.02 us: gather_rows(): return lax.all_gather(values, axes, axis=0, tiled=True)]
    psum x10 -> x0, blocking collectives: 350 us -> none  [the longest x4 160 us: normalize(): lax.psum((jnp.sum(values, axis=0), jnp.sum(values * values, axis=0)), ('g...]
    psum x2 -> x0, waiting for transfers between devices: 152 us -> none  [the longest x1 118 us: shards(): lax.psum((grad_enc_mid, grad_latent_w, grad_dec_in, decoder_middle_gradie...]
    reduce_scatter x2 -> x0, waiting for transfers between devices: 150 us -> none  [the longest x1 76.7 us: shards(): lax.psum_scatter(jnp.dot(block, encoder_input_reduced, preferred_element_...]
    ppermute x0 -> x62, waiting for transfers between devices: none -> 146 us  [swap(): return lax.ppermute(values, axis, pairs)]
    pallas_call x0 -> x3, Pallas kernels: none -> 104 us  [on_chip(): pl.pallas_call(kernel, out_shape=shape, in_specs=[scalars if operand.dtyp...]
  transfers between devices with their start and end apart: 16 -> 65, of which waited for: 15 -> 29; matrix products, arithmetic and copies ran while one was open for 18% -> 20% of each run, Pallas kernels for 0% -> 11%
where the time goes in v1:
time: 486 us; the launch traced here: 478 us
  waiting for transfers between devices  146 us (30%)
  Pallas kernels  104 us (21%)
  matrix products  58.9 us (12%)
  other arithmetic  55.8 us (11%)
  starting transfers between devices  52.2 us (11%)
  local copies, waits for them, and re-layouts  41.7 us (9%)
  between operations  19.7 us (4%)
    ppermute x62, waiting for transfers between devices, swap(): return lax.ppermute(values, axis, pairs)  146 us
    pallas_call x3, Pallas kernels, on_chip(): pl.pallas_call(kernel, out_shape=shape, in_specs=[scalars if operand.dtyp...  104 us
    ppermute x62, starting transfers between devices, swap(): return lax.ppermute(values, axis, pairs)  51.7 us
    dot_general x7, matrix products, inner_rows(): lax.dot_general(left, right, (((0,), (0,)), ((), ())), preferred_element_...  23.6 us
    dot_general x5, matrix products, outer_cols(): lax.dot_general(left, right, (((1,), (1,)), ((), ())), preferred_element_...  21.9 us
    convert_element_type x11, other arithmetic, low(): return values.astype(jnp.bfloat16)  17.3 us
    dot_general x8, matrix products, rows_times(): return jnp.dot(left, right, preferred_element_type=jnp.float32)  13.5 us
  transfers between devices with their start and end apart: 65, of which 29 were waited for; matrix products, arithmetic and copies ran while one was open for 20% of the time, Pallas kernels for 11%

profile of v1, /device:TPU:0, one launch (start us, length us, event | category | flops | bytes accessed | tf_op | source)
XLA Modules:
  0.0 478.0 jit_solution(6553926958399975219)
XLA Ops:
  7.3 3.0 collective-permute-start
  10.3 1.6 collective-permute-start.1
  11.9 2.6 collective-permute-start.3
  15.8 2.6 collective-permute-start.18
  23.5 2.3 broadcast_in_dim.31
  27.4 14.8 %collective-permute-done.7 = bf16[56,800]{1,0:T(8,128)(2,1)S(1)} collective-permute-done((bf16[56,800]{1,0:T(8,128)(2,1)S(1)}, bf16[56,800]{1,0:T(8,128)(2,1)S(1)}, u32[]{:S(2)}, u32[]{:S(2)}) %collective-permute-start.7) | collective-permute-done | bytes 89632 | tf_op jit(solution)/shard_map/ppermute | solution.py:51
  43.3 5.7 %collective-permute-done.8 = bf16[2,56,800]{2,1,0:T(8,128)(2,1)S(1)} collective-permute-done((bf16[2,56,800]{2,1,0:T(8,128)(2,1)S(1)}, bf16[2,56,800]{2,1,0:T(8,128)(2,1)S(1)}, u32[]{:S(2)}, u32[]{:S(2)}) %collective-permute-start.8) | collective-permute-done | bytes 179232 | tf_op jit(solution)/shard_map/ppermute | solution.py:51
  50.5 8.2 %collective-permute-done.9 = bf16[2,2,56,800]{3,2,1,0:T(8,128)(2,1)S(1)} collective-permute-done((bf16[2,2,56,800]{3,2,1,0:T(8,128)(2,1)S(1)}, bf16[2,2,56,800]{3,2,1,0:T(8,128)(2,1)S(1)}, u32[]{:S(2)}, u32[]{:S(2)}) %collective-permute-start.9) | collective-permute-done | bytes 358432 | tf_op jit(solution)/shard_map/ppermute | solution.py:51
  59.0 1.6 collective-permute-start.10
  61.2 2.2 collective-permute-start.5
  64.7 1.6 collective-permute-start.2
  66.8 5.4 %collective-permute-done.5 = bf16[224,1024]{1,0:T(8,128)(2,1)S(1)} collective-permute-done((bf16[224,1024]{1,0:T(8,128)(2,1)S(1)}, bf16[224,1024]{1,0:T(8,128)(2,1)S(1)}, u32[]{:S(2)}, u32[]{:S(2)}) %collective-permute-start.5) | collective-permute-done | bytes 458784 | tf_op jit(solution)/shard_map/ppermute | solution.py:51
  73.2 1.8 bitcast_dynamic-update-slice_fusion.7
  76.0 1.9 bitcast_dynamic-update-slice_fusion.6
  77.9 8.2 %collective-permute-done.2 = bf16[224,1024]{1,0:T(8,128)(2,1)S(1)} collective-permute-done((bf16[224,1024]{1,0:T(8,128)(2,1)}, bf16[224,1024]{1,0:T(8,128)(2,1)S(1)}, u32[]{:S(2)}, u32[]{:S(2)}) %collective-permute-start.2) | collective-permute-done | bytes 458784 | tf_op jit(solution)/shard_map/ppermute | solution.py:51
  87.8 8.1 %collective-permute-done.4 = bf16[224,1024]{1,0:T(8,128)(2,1)S(1)} collective-permute-done((bf16[224,1024]{1,0:T(8,128)(2,1)S(1)}, bf16[224,1024]{1,0:T(8,128)(2,1)S(1)}, u32[]{:S(2)}, u32[]{:S(2)}) %collective-permute-start.4) | collective-permute-done | bytes 458784 | tf_op jit(solution)/shard_map/ppermute | solution.py:51
  97.5 3.3 collective-permute-done.6
  102.6 5.5 %fusion.123 = (f32[800]{0:T(1024)S(1)}, f32[800]{0:T(1024)S(1)}, f32[1024,800]{0,1:T(8,128)S(1)}) fusion(bf16[1792,1024]{1,0:T(8,128)(2,1)} %bitcast.9, bf16[1792,800]{1,0:T(8,128)(2,1)S(1)} %bitcast.220), kind=kOutput, calls=%fused_computation.337 | convolution fusion | flops 2938468864 | bytes 9820416 | tf_op jit(solution)/shard_map/dot_general | solution.py:24
  110.2 1.8 collective-permute-done.13
  113.3 2.0 fusion.31
  115.3 2.1 fusion.122
  120.6 2.1 reshape_reshape.7
  123.3 1.8 fusion.39
  125.6 1.9 subtract_reduce_fusion
  130.4 2.1 collective-permute-done.22
  134.1 1.8 fusion.47
  135.9 2.2 fusion.120
  143.9 3.1 fusion.55
  148.3 2.3 fusion.78
  150.9 7.6 %multiply_convert_fusion = (bf16[1792,1024]{1,0:T(8,128)(2,1)S(1)}, f32[]{:T(128)}) fusion(f32[1792,1024]{1,0:T(8,128)S(1)} %fusion.78, f32[1792]{0:T(1024)S(1)} %convert_reduce_fusion.1, bf16[8,224,1024]{2,1,0:T(8,128)(2,1)} %bitcast_dynamic-update-slice_fusion.1, bf16[1024,800]{0,1:T(8,128)(2,1)S(1)} %copy-done.11, bf16[1792,811]{1,0:T(8,128)(2,1)S(1)} %copy-done.48), kind=kOutput, calls=%fused_computation.1 | convolution fusion | flops 2950692864 | bytes 19232260 | tf_op jit(solution)/shard_map/dot_general | solution.py:30
  158.5 7.4 %fusion.119 = (f32[800]{0:T(1024)S(1)}, f32[800]{0:T(1024)S(1)}, f32[1024,800]{0,1:T(8,128)}) fusion(f32[800]{0:T(1024)S(1)} %copy-done.58, f32[1024,800]{0,1:T(8,128)S(1)} %copy-done.10, f32[800]{0:T(1024)S(1)} %get-tuple-element.39, f32[800]{0:T(1024)S(1)} %copy-done.79, f32[800]{0:T(1024)S(1)} %copy-done.67, ...), kind=kOutput, calls=%fused_computation.333 | convolution fusion | flops 2957310464 | bytes 13149440 | tf_op jit(solution)/shard_map/dot_general | solution.py:24
  168.4 1.6 fusion.80
  175.5 3.9 multiply_convert_fusion.4
  179.4 4.1 fusion.118
  189.2 2.1 multiply_convert_fusion.3
  191.3 3.5 collective-permute-done.28
  194.8 3.2 collective-permute-done.29
  198.7 2.4 add_convert_fusion.1
  201.2 3.6 fusion.117
  207.1 2.2 collective-permute-done.40
  213.6 4.2 fusion.116
  219.8 1.8 collective-permute-done.43
  225.5 6.0 %collective-permute-done.46 = f32[56,800]{1,0:T(8,128)S(1)} collective-permute-done((f32[56,800]{1,0:T(8,128)S(1)}, f32[56,800]{1,0:T(8,128)S(1)}, u32[]{:S(2)}, u32[]{:S(2)}) %collective-permute-start.46) | collective-permute-done | bytes 179232 | tf_op jit(solution)/shard_map/ppermute | solution.py:51
  231.5 3.2 collective-permute-done.47
  236.7 2.1 fusion.63
  240.9 3.9 fusion.125
  253.6 3.8 fusion.124
  259.5 10.5 %collective-permute-done.59 = f32[80,800]{1,0:T(8,128)S(1)} collective-permute-done((f32[80,800]{1,0:T(8,128)S(1)}, f32[80,800]{1,0:T(8,128)S(1)}, u32[]{:S(2)}, u32[]{:S(2)}) %collective-permute-start.59) | collective-permute-done | bytes 256032 | tf_op jit(solution)/shard_map/ppermute | solution.py:51
  276.0 3.8 collective-permute-done.60
  279.8 21.1 %collective-permute-done.54 = f32[200,800]{1,0:T(8,128)S(1)} collective-permute-done((f32[200,800]{1,0:T(8,128)S(1)}, f32[200,800]{1,0:T(8,128)S(1)}, u32[]{:S(2)}, u32[]{:S(2)}) %collective-permute-start.54) | collective-permute-done | bytes 640032 | tf_op jit(solution)/shard_map/ppermute | solution.py:51
  302.6 14.7 %collective-permute-done.50 = f32[200,800]{1,0:T(8,128)S(1)} collective-permute-done((f32[200,800]{1,0:T(8,128)S(1)}, f32[200,800]{1,0:T(8,128)S(1)}, u32[]{:S(2)}, u32[]{:S(2)}) %collective-permute-start.50) | collective-permute-done | bytes 640032 | tf_op jit(solution)/shard_map/ppermute | solution.py:51
  317.4 2.1 collective-permute-start.51
  319.5 6.2 %collective-permute-done.55 = bf16[200,800]{1,0:T(8,128)(2,1)S(1)} collective-permute-done((bf16[200,800]{1,0:T(8,128)(2,1)S(1)}, bf16[200,800]{1,0:T(8,128)(2,1)S(1)}, u32[]{:S(2)}, u32[]{:S(2)}) %collective-permute-start.55) | collective-permute-done | bytes 320032 | tf_op jit(solution)/shard_map/ppermute | solution.py:51
  325.9 6.2 %collective-permute-done.51 = bf16[200,800]{1,0:T(8,128)(2,1)S(1)} collective-permute-done((bf16[200,800]{1,0:T(8,128)(2,1)S(1)}, bf16[200,800]{1,0:T(8,128)(2,1)S(1)}, u32[]{:S(2)}, u32[]{:S(2)}) %collective-permute-start.51) | collective-permute-done | bytes 320032 | tf_op jit(solution)/shard_map/ppermute | solution.py:51
  332.9 1.6 collective-permute-done.52
  335.6 2.4 convert_add_fusion
  338.0 31.5 %shard_map.400 = bf16[800,800]{1,0:T(8,128)(2,1)} custom-call(s32[1]{0:T(128)} %bitcast.46.place, f32[800,800]{1,0:T(8,128)S(1)} %get-tuple-element.231.even, f32[800,800]{1,0:T(8,128)} %get-tuple-element.230.odd), custom_call_target="tpu_custom_call" | custom-call | flops 15360000000 | bytes 4194304 | tf_op jit(solution)/shard_map/pallas_call | solution.py:315
  370.9 23.1 %shard_map.401 = f32[3,100,800]{2,1,0:T(8,128)S(1)} custom-call(f32[3,100,800]{2,1,0:T(8,128)S(1)} %pad_maximum_fusion.5.moments), custom_call_target="tpu_custom_call" | custom-call | flops 3060000000 | bytes 4194304 | tf_op jit(solution)/shard_map/pallas_call | solution.py:315
  397.4 5.1 %multiply_subtract_fusion = (f32[800,800]{1,0:T(8,128)}, f32[800,800]{1,0:T(8,128)}) fusion(f32[800,800]{1,0:T(8,128)S(1)} %copy-done.26, bf16[800,800]{1,0:T(8,128)(2,1)} %shard_map.400, bf16[800,800]{1,0:T(8,128)(2,1)} %collective-permute-done.57, pred[]{:T(512)S(6)} %ne.10, f32[800,800]{1,0:T(8,128)S(1)} %copy-done.23), kind=kLoop, calls=%fused_computation.90 | loop fusion | flops 5120000 | bytes 12800001 | tf_op jit(solution)/shard_map/sub | solution.py:553
  402.5 1.9 dynamic-slice_convert_fusion
  405.7 6.0 %slice.203 = f32[32,56,800]{2,1,0:T(8,128)} slice(f32[32,64,800]{2,1,0:T(8,128)} %bitcast.215), slice={[0:32], [0:56], [0:800]} | slice | bytes 11468800 | tf_op jit(solution)/shard_map/slice | solution.py:156
  412.3 1.9 copy-done.1
  414.2 49.0 %shard_map.399 = bf16[224,800]{1,0:T(8,128)(2,1)S(1)} custom-call(s32[2]{0:T(128)S(1)} %pad_add_fusion.place, bf16[1792,800]{1,0:T(8,128)(2,1)S(1)} %copy-done.1, f32[1792,800]{1,0:T(8,128)} %bitcast.211), custom_call_target="tpu_custom_call" | custom-call | flops 28057600000 | bytes 4194304 | tf_op jit(solution)/shard_map/pallas_call | solution.py:315
  465.4 2.1 dynamic-slice_bitcast_fusion
  (473 shorter events, 99.4 us)
Async XLA Ops:
  7.2 139.7 %all-gather.6.cloned.1.call-start = ((), (), s32[]{:S(2)}) async-start(), calls=%async_computation | async-start | bytes 3311616 | tf_op jit(solution)/shard_map/all_gather | solution.py:183
  7.3 56.9 %collective-permute-start = (bf16[224,1024]{1,0:T(8,128)(2,1)}, bf16[224,1024]{1,0:T(8,128)(2,1)}, u32[]{:S(2)}, u32[]{:S(2)}) collective-permute-start(bf16[224,1024]{1,0:T(8,128)(2,1)} %bitcast.227), channel_id=1, source_target_pairs={{0,4},{4,0},{8,12},{12,8},{16,20},{20,16},{24,28},{28,24},{1,5},{5... | collective-permute-start | bytes 1376264 | tf_op jit(solution)/shard_map/ppermute | solution.py:51
  10.3 54.4 %collective-permute-start.1 = (bf16[224,1024]{1,0:T(8,128)(2,1)}, bf16[224,1024]{1,0:T(8,128)(2,1)}, u32[]{:S(2)}, u32[]{:S(2)}) collective-permute-start(bf16[224,1024]{1,0:T(8,128)(2,1)} %bitcast.228), channel_id=1, source_target_pairs={{0,8},{4,12},{8,0},{12,4},{16,24},{20,28},{24,16},{28,20},{1,9},{5... | collective-permute-start | bytes 1376264 | tf_op jit(solution)/shard_map/ppermute | solution.py:51
  11.9 54.4 %collective-permute-start.3 = (bf16[224,1024]{1,0:T(8,128)(2,1)}, bf16[224,1024]{1,0:T(8,128)(2,1)S(1)}, u32[]{:S(2)}, u32[]{:S(2)}) collective-permute-start(bf16[224,1024]{1,0:T(8,128)(2,1)} %bitcast.229), channel_id=1, source_target_pairs={{0,16},{4,20},{8,24},{12,28},{16,0},{20,4},{24,8},{28,12},{1,17},{... | collective-permute-start | bytes 1376264 | tf_op jit(solution)/shard_map/ppermute | solution.py:51
  15.4 26.8 %collective-permute-start.7 = (bf16[56,800]{1,0:T(8,128)(2,1)S(1)}, bf16[56,800]{1,0:T(8,128)(2,1)S(1)}, u32[]{:S(2)}, u32[]{:S(2)}) collective-permute-start(bf16[56,800]{1,0:T(8,128)(2,1)S(1)} %dynamic-slice_convert_fusion.1), channel_id=1, source_target_pairs={{0,16},{4,20},{8,24},{12,28},{16,0},{20,4},{24,8},{28,12},{1,17},{... | collective-permute-start | bytes 268808 | tf_op jit(solution)/shard_map/ppermute | solution.py:51
  15.8 33.8 %collective-permute-start.18 = (f32[128,100]{0,1:T(8,128)}, f32[128,100]{0,1:T(8,128)}, u32[]{:S(2)}, u32[]{:S(2)}) collective-permute-start(f32[128,100]{0,1:T(8,128)} %param.27), channel_id=1, source_target_pairs={{0,16},{4,20},{8,24},{12,28},{16,0},{20,4},{24,8},{28,12},{1,17},{... | collective-permute-start | bytes 153608 | tf_op jit(solution)/shard_map/ppermute | solution.py:51
  22.3 380.2 %all-gather.8.cloned.1.call-start = ((), (), s32[]{:S(2)}) async-start(), calls=%async_computation.1 | async-start | bytes 3311616 | tf_op jit(solution)/shard_map/all_gather | solution.py:152
  43.2 5.8 %collective-permute-start.8 = (bf16[2,56,800]{2,1,0:T(8,128)(2,1)S(1)}, bf16[2,56,800]{2,1,0:T(8,128)(2,1)S(1)}, u32[]{:S(2)}, u32[]{:S(2)}) collective-permute-start(bf16[2,56,800]{2,1,0:T(8,128)(2,1)S(1)} %pad_maximum_fusion.14), channel_id=1, source_target_pairs={{0,8},{4,12},{8,0},{12,4},{16,24},{20,28},{24,16},{28,20},{1,9},{5... | collective-permute-start | bytes 537608 | tf_op jit(solution)/shard_map/ppermute | solution.py:51
  49.1 9.7 %collective-permute-start.9 = (bf16[2,2,56,800]{3,2,1,0:T(8,128)(2,1)S(1)}, bf16[2,2,56,800]{3,2,1,0:T(8,128)(2,1)S(1)}, u32[]{:S(2)}, u32[]{:S(2)}) collective-permute-start(bf16[2,2,56,800]{3,2,1,0:T(8,128)(2,1)S(1)} %pad_maximum_fusion.12), channel_id=1, source_target_pairs={{0,4},{4,0},{8,12},{12,8},{16,20},{20,16},{24,28},{28,24},{1,5},{5... | collective-permute-start | bytes 1075208 | tf_op jit(solution)/shard_map/ppermute | solution.py:51
  50.5 10.8 %collective-permute-start.19 = (f32[2,128,100]{1,2,0:T(8,128)S(1)}, f32[2,128,100]{1,2,0:T(8,128)S(1)}, u32[]{:S(2)}, u32[]{:S(2)}) collective-permute-start(f32[2,128,100]{1,2,0:T(8,128)S(1)} %pad_maximum_fusion.15), channel_id=1, source_target_pairs={{0,8},{4,12},{8,0},{12,4},{16,24},{20,28},{24,16},{28,20},{1,9},{5... | collective-permute-start | bytes 307208 | tf_op jit(solution)/shard_map/ppermute | solution.py:51
  59.0 16.5 %collective-permute-start.10 = (bf16[8,56,800]{2,1,0:T(8,128)(2,1)S(1)}, bf16[8,56,800]{2,1,0:T(8,128)(2,1)S(1)}, u32[]{:S(2)}, u32[]{:S(2)}) collective-permute-start(bf16[8,56,800]{2,1,0:T(8,128)(2,1)S(1)} %bitcast.222), channel_id=1, source_target_pairs={{0,2},{1,3},{2,0},{3,1},{4,6},{5,7},{6,4},{7,5},{8,10},{9,11},{10,... | collective-permute-start | bytes 2150408 | tf_op jit(solution)/shard_map/ppermute | solution.py:51
  61.2 10.9 %collective-permute-start.5 = (bf16[224,1024]{1,0:T(8,128)(2,1)S(1)}, bf16[224,1024]{1,0:T(8,128)(2,1)S(1)}, u32[]{:S(2)}, u32[]{:S(2)}) collective-permute-start(bf16[224,1024]{1,0:T(8,128)(2,1)S(1)} %bitcast.230), channel_id=1, source_target_pairs={{0,24},{4,28},{8,16},{12,20},{16,8},{20,12},{24,0},{28,4},{1,25},{... | collective-permute-start | bytes 1376264 | tf_op jit(solution)/shard_map/ppermute | solution.py:51
  64.2 46.0 %collective-permute-start.20 = (f32[2,2,128,100]{2,3,0,1:T(8,128)S(1)}, f32[2,2,128,100]{2,3,0,1:T(8,128)S(1)}, u32[]{:S(2)}, u32[]{:S(2)}) collective-permute-start(f32[2,2,128,100]{2,3,0,1:T(8,128)S(1)} %pad_maximum_fusion.13), channel_id=1, source_target_pairs={{0,4},{4,0},{8,12},{12,8},{16,20},{20,16},{24,28},{28,24},{1,5},{5... | collective-permute-start | bytes 614408 | tf_op jit(solution)/shard_map/ppermute | solution.py:51
  64.7 21.4 %collective-permute-start.2 = (bf16[224,1024]{1,0:T(8,128)(2,1)}, bf16[224,1024]{1,0:T(8,128)(2,1)S(1)}, u32[]{:S(2)}, u32[]{:S(2)}) collective-permute-start(bf16[224,1024]{1,0:T(8,128)(2,1)} %collective-permute-done.1), channel_id=1, source_target_pairs={{0,4},{4,0},{8,12},{12,8},{16,20},{20,16},{24,28},{28,24},{1,5},{5... | collective-permute-start | bytes 1376264 | tf_op jit(solution)/shard_map/ppermute | solution.py:51
  66.3 29.5 %collective-permute-start.4 = (bf16[224,1024]{1,0:T(8,128)(2,1)S(1)}, bf16[224,1024]{1,0:T(8,128)(2,1)S(1)}, u32[]{:S(2)}, u32[]{:S(2)}) collective-permute-start(bf16[224,1024]{1,0:T(8,128)(2,1)S(1)} %collective-permute-done.3), channel_id=1, source_target_pairs={{0,4},{4,0},{8,12},{12,8},{16,20},{20,16},{24,28},{28,24},{1,5},{5... | collective-permute-start | bytes 1376264 | tf_op jit(solution)/shard_map/ppermute | solution.py:51
  72.2 28.6 %collective-permute-start.6 = (bf16[224,1024]{1,0:T(8,128)(2,1)S(1)}, bf16[224,1024]{1,0:T(8,128)(2,1)S(1)}, u32[]{:S(2)}, u32[]{:S(2)}) collective-permute-start(bf16[224,1024]{1,0:T(8,128)(2,1)S(1)} %collective-permute-done.5), channel_id=1, source_target_pairs={{0,4},{4,0},{8,12},{12,8},{16,20},{20,16},{24,28},{28,24},{1,5},{5... | collective-permute-start | bytes 1376264 | tf_op jit(solution)/shard_map/ppermute | solution.py:51
  75.9 25.6 %collective-permute-start.11 = (bf16[8,2,56,800]{3,2,0,1:T(8,128)(2,1)S(1)}, bf16[8,2,56,800]{3,2,0,1:T(8,128)(2,1)S(1)}, u32[]{:S(2)}, u32[]{:S(2)}) collective-permute-start(bf16[8,2,56,800]{3,2,0,1:T(8,128)(2,1)S(1)} %pad_maximum_fusion.1), channel_id=1, source_target_pairs={{0,1},{1,0},{2,3},{3,2},{4,5},{5,4},{6,7},{7,6},{8,9},{9,8},{10,11... | collective-permute-start | bytes 4300808 | tf_op jit(solution)/shard_map/ppermute | solution.py:51
  108.2 2.0 collective-permute-start.12
  108.3 3.7 collective-permute-start.13
  108.9 3.1 collective-permute-start.14
  117.5 5.2 %collective-permute-start.15 = (f32[2,800]{1,0:T(2,128)S(1)}, f32[2,800]{1,0:T(2,128)S(1)}, u32[]{:S(2)}, u32[]{:S(2)}) collective-permute-start(f32[2,800]{1,0:T(2,128)S(1)} %pad_maximum_fusion.19), channel_id=1, source_target_pairs={{0,1},{1,0},{2,3},{3,2},{4,5},{5,4},{6,7},{7,6},{8,9},{9,8},{10,11... | collective-permute-start | bytes 19208 | tf_op jit(solution)/shard_map/ppermute | solution.py:51
  117.7 5.0 %collective-permute-start.16 = (f32[2,800]{1,0:T(2,128)S(1)}, f32[2,800]{1,0:T(2,128)S(1)}, u32[]{:S(2)}, u32[]{:S(2)}) collective-permute-start(f32[2,800]{1,0:T(2,128)S(1)} %pad_maximum_fusion.19), channel_id=1, source_target_pairs={{0,2},{1,3},{2,0},{3,1},{4,6},{5,7},{6,4},{7,5},{8,10},{9,11},{10,... | collective-permute-start | bytes 19208 | tf_op jit(solution)/shard_map/ppermute | solution.py:51
  119.2 3.5 collective-permute-start.17
  128.4 2.0 collective-permute-start.21
  128.9 3.6 collective-permute-start.22
  130.3 3.1 collective-permute-start.23
  138.2 2.6 collective-permute-start.24
  138.3 3.6 collective-permute-start.25
  139.0 3.1 collective-permute-start.26
  166.5 7.5 %collective-permute-start.30 = (f32[2,800]{1,0:T(2,128)}, f32[2,800]{1,0:T(2,128)}, u32[]{:S(2)}, u32[]{:S(2)}) collective-permute-start(f32[2,800]{1,0:T(2,128)} %pad_maximum_fusion.22), channel_id=1, source_target_pairs={{0,1},{1,0},{2,3},{3,2},{4,5},{5,4},{6,7},{7,6},{8,9},{9,8},{10,11... | collective-permute-start | bytes 19208 | tf_op jit(solution)/shard_map/ppermute | solution.py:51
  166.6 7.4 %collective-permute-start.31 = (f32[2,800]{1,0:T(2,128)}, f32[2,800]{1,0:T(2,128)}, u32[]{:S(2)}, u32[]{:S(2)}) collective-permute-start(f32[2,800]{1,0:T(2,128)} %pad_maximum_fusion.22), channel_id=1, source_target_pairs={{0,2},{1,3},{2,0},{3,1},{4,6},{5,7},{6,4},{7,5},{8,10},{9,11},{10,... | collective-permute-start | bytes 19208 | tf_op jit(solution)/shard_map/ppermute | solution.py:51
  168.1 6.0 %collective-permute-start.32 = (f32[2,800]{1,0:T(2,128)}, f32[2,800]{1,0:T(2,128)}, u32[]{:S(2)}, u32[]{:S(2)}) collective-permute-start(f32[2,800]{1,0:T(2,128)} %pad_maximum_fusion.22), channel_id=1, source_target_pairs={{0,3},{1,2},{2,1},{3,0},{4,7},{5,6},{6,5},{7,4},{8,11},{9,10},{10,... | collective-permute-start | bytes 19208 | tf_op jit(solution)/shard_map/ppermute | solution.py:51
  183.6 4.1 collective-permute-start.33
  184.1 3.7 collective-permute-start.34
  185.5 3.1 collective-permute-start.35
  185.6 5.7 %collective-permute-start.27 = (f32[64,800]{1,0:T(8,128)S(1)}, f32[64,800]{1,0:T(8,128)S(1)}, u32[]{:S(2)}, u32[]{:S(2)}) collective-permute-start(f32[64,800]{1,0:T(8,128)S(1)} %get-tuple-element.162), channel_id=1, source_target_pairs={{0,1},{1,0},{2,3},{3,2},{4,5},{5,4},{6,7},{7,6},{8,9},{9,8},{10,11... | collective-permute-start | bytes 614408 | tf_op jit(solution)/shard_map/ppermute | solution.py:51
  186.3 8.5 %collective-permute-start.28 = (f32[64,800]{1,0:T(8,128)S(1)}, f32[64,800]{1,0:T(8,128)S(1)}, u32[]{:S(2)}, u32[]{:S(2)}) collective-permute-start(f32[64,800]{1,0:T(8,128)S(1)} %get-tuple-element.161), channel_id=1, source_target_pairs={{0,2},{1,3},{2,0},{3,1},{4,6},{5,7},{6,4},{7,5},{8,10},{9,11},{10,... | collective-permute-start | bytes 614408 | tf_op jit(solution)/shard_map/ppermute | solution.py:51
  187.7 10.2 %collective-permute-start.29 = (f32[64,800]{1,0:T(8,128)S(1)}, f32[64,800]{1,0:T(8,128)S(1)}, u32[]{:S(2)}, u32[]{:S(2)}) collective-permute-start(f32[64,800]{1,0:T(8,128)S(1)} %get-tuple-element.160), channel_id=1, source_target_pairs={{0,3},{1,2},{2,1},{3,0},{4,7},{5,6},{6,5},{7,4},{8,11},{9,10},{10,... | collective-permute-start | bytes 614408 | tf_op jit(solution)/shard_map/ppermute | solution.py:51
  204.9 2.3 collective-permute-start.39
  205.7 3.6 collective-permute-start.40
  207.1 3.1 collective-permute-start.41
  218.0 3.6 collective-permute-start.43
  218.7 3.1 collective-permute-start.44
  223.5 2.0 collective-permute-start.45
  223.7 7.8 %collective-permute-start.46 = (f32[56,800]{1,0:T(8,128)S(1)}, f32[56,800]{1,0:T(8,128)S(1)}, u32[]{:S(2)}, u32[]{:S(2)}) collective-permute-start(f32[56,800]{1,0:T(8,128)S(1)} %get-tuple-element.166), channel_id=1, source_target_pairs={{0,2},{1,3},{2,0},{3,1},{4,6},{5,7},{6,4},{7,5},{8,10},{9,11},{10,... | collective-permute-start | bytes 537608 | tf_op jit(solution)/shard_map/ppermute | solution.py:51
  225.1 9.6 %collective-permute-start.47 = (f32[56,800]{1,0:T(8,128)S(1)}, f32[56,800]{1,0:T(8,128)S(1)}, u32[]{:S(2)}, u32[]{:S(2)}) collective-permute-start(f32[56,800]{1,0:T(8,128)S(1)} %get-tuple-element.165), channel_id=1, source_target_pairs={{0,3},{1,2},{2,1},{3,0},{4,7},{5,6},{6,5},{7,4},{8,11},{9,10},{10,... | collective-permute-start | bytes 537608 | tf_op jit(solution)/shard_map/ppermute | solution.py:51
  235.4 169.0 %all-gather.10.cloned.1.call-start = ((), (), s32[]{:S(2)}) async-start(), calls=%async_computation.2 | async-start | bytes 7569408 | tf_op jit(solution)/shard_map/all_gather | solution.py:152
  246.0 25.4 %collective-permute-start.53 = (f32[400,800]{1,0:T(8,128)}, f32[400,800]{1,0:T(8,128)}, u32[]{:S(2)}, u32[]{:S(2)}) collective-permute-start(f32[400,800]{1,0:T(8,128)} %constant_dynamic-slice_fusion.4), channel_id=1, source_target_pairs={{0,1},{1,0},{2,3},{3,2},{4,5},{5,4},{6,7},{7,6},{8,9},{9,8},{10,11... | collective-permute-start | bytes 3840008 | tf_op jit(solution)/shard_map/ppermute | solution.py:51
  246.6 4.7 collective-permute-start.36
  246.7 4.6 collective-permute-start.37
  248.1 3.3 collective-permute-start.38
  250.9 6.9 %collective-permute-start.58 = (f32[160,800]{1,0:T(8,128)}, f32[160,800]{1,0:T(8,128)S(1)}, u32[]{:S(2)}, u32[]{:S(2)}) collective-permute-start(f32[160,800]{1,0:T(8,128)} %constant_dynamic-slice_fusion.2), channel_id=1, source_target_pairs={{0,1},{1,0},{2,3},{3,2},{4,5},{5,4},{6,7},{7,6},{8,9},{9,8},{10,11... | collective-permute-start | bytes 1536008 | tf_op jit(solution)/shard_map/ppermute | solution.py:51
  257.6 16.2 %collective-permute-start.49 = (f32[400,800]{1,0:T(8,128)S(1)}, f32[400,800]{1,0:T(8,128)S(1)}, u32[]{:S(2)}, u32[]{:S(2)}) collective-permute-start(f32[400,800]{1,0:T(8,128)S(1)} %constant_dynamic-slice_fusion.6), channel_id=1, source_target_pairs={{0,1},{1,0},{2,3},{3,2},{4,5},{5,4},{6,7},{7,6},{8,9},{9,8},{10,11... | collective-permute-start | bytes 3840008 | tf_op jit(solution)/shard_map/ppermute | solution.py:51
  257.9 12.0 %collective-permute-start.59 = (f32[80,800]{1,0:T(8,128)S(1)}, f32[80,800]{1,0:T(8,128)S(1)}, u32[]{:S(2)}, u32[]{:S(2)}) collective-permute-start(f32[80,800]{1,0:T(8,128)S(1)} %constant_dynamic-slice_fusion.1), channel_id=1, source_target_pairs={{0,2},{1,3},{2,0},{3,1},{4,6},{5,7},{6,4},{7,5},{8,10},{9,11},{10,... | collective-permute-start | bytes 768008 | tf_op jit(solution)/shard_map/ppermute | solution.py:51
  270.0 9.8 %collective-permute-start.60 = (f32[80,800]{1,0:T(8,128)S(1)}, f32[80,800]{1,0:T(8,128)S(1)}, u32[]{:S(2)}, u32[]{:S(2)}) collective-permute-start(f32[80,800]{1,0:T(8,128)S(1)} %dynamic-slice_add_fusion.3), channel_id=1, source_target_pairs={{0,2},{1,3},{2,0},{3,1},{4,6},{5,7},{6,4},{7,5},{8,10},{9,11},{10,... | collective-permute-start | bytes 768008 | tf_op jit(solution)/shard_map/ppermute | solution.py:51
  273.0 28.0 %collective-permute-start.54 = (f32[200,800]{1,0:T(8,128)S(1)}, f32[200,800]{1,0:T(8,128)S(1)}, u32[]{:S(2)}, u32[]{:S(2)}) collective-permute-start(f32[200,800]{1,0:T(8,128)S(1)} %constant_dynamic-slice_fusion.3), channel_id=1, source_target_pairs={{0,2},{1,3},{2,0},{3,1},{4,6},{5,7},{6,4},{7,5},{8,10},{9,11},{10,... | collective-permute-start | bytes 1920008 | tf_op jit(solution)/shard_map/ppermute | solution.py:51
  274.0 43.3 %collective-permute-start.50 = (f32[200,800]{1,0:T(8,128)S(1)}, f32[200,800]{1,0:T(8,128)S(1)}, u32[]{:S(2)}, u32[]{:S(2)}) collective-permute-start(f32[200,800]{1,0:T(8,128)S(1)} %constant_dynamic-slice_fusion.5), channel_id=1, source_target_pairs={{0,2},{1,3},{2,0},{3,1},{4,6},{5,7},{6,4},{7,5},{8,10},{9,11},{10,... | collective-permute-start | bytes 1920008 | tf_op jit(solution)/shard_map/ppermute | solution.py:51
  301.0 24.6 %collective-permute-start.55 = (bf16[200,800]{1,0:T(8,128)(2,1)S(1)}, bf16[200,800]{1,0:T(8,128)(2,1)S(1)}, u32[]{:S(2)}, u32[]{:S(2)}) collective-permute-start(bf16[200,800]{1,0:T(8,128)(2,1)S(1)} %reduce-precision_convert_fusion), channel_id=1, source_target_pairs={{0,2},{1,3},{2,0},{3,1},{4,6},{5,7},{6,4},{7,5},{8,10},{9,11},{10,... | collective-permute-start | bytes 960008 | tf_op jit(solution)/shard_map/ppermute | solution.py:51
  302.5 29.8 %collective-permute-start.61 = (f32[160,800]{1,0:T(8,128)S(1)}, f32[160,800]{1,0:T(8,128)S(1)}, u32[]{:S(2)}, u32[]{:S(2)}) collective-permute-start(f32[160,800]{1,0:T(8,128)S(1)} %bitcast.226), channel_id=1, source_target_pairs={{0,1},{1,0},{2,3},{3,2},{4,5},{5,4},{6,7},{7,6},{8,9},{9,8},{10,11... | collective-permute-start | bytes 1536008 | tf_op jit(solution)/shard_map/ppermute | solution.py:51
  317.4 14.7 %collective-permute-start.51 = (bf16[200,800]{1,0:T(8,128)(2,1)S(1)}, bf16[200,800]{1,0:T(8,128)(2,1)S(1)}, u32[]{:S(2)}, u32[]{:S(2)}) collective-permute-start(bf16[200,800]{1,0:T(8,128)(2,1)S(1)} %reduce-precision_convert_fusion.1), channel_id=1, source_target_pairs={{0,2},{1,3},{2,0},{3,1},{4,6},{5,7},{6,4},{7,5},{8,10},{9,11},{10,... | collective-permute-start | bytes 960008 | tf_op jit(solution)/shard_map/ppermute | solution.py:51
  325.8 6.7 %collective-permute-start.56 = (bf16[400,800]{1,0:T(8,128)(2,1)S(1)}, bf16[400,800]{1,0:T(8,128)(2,1)S(1)}, u32[]{:S(2)}, u32[]{:S(2)}) collective-permute-start(bf16[400,800]{1,0:T(8,128)(2,1)S(1)} %bitcast.224), channel_id=1, source_target_pairs={{0,1},{1,0},{2,3},{3,2},{4,5},{5,4},{6,7},{7,6},{8,9},{9,8},{10,11... | collective-permute-start | bytes 1920008 | tf_op jit(solution)/shard_map/ppermute | solution.py:51
  332.2 2.3 collective-permute-start.52
  369.5 27.9 %collective-permute-start.57 = (bf16[800,800]{1,0:T(8,128)(2,1)}, bf16[800,800]{1,0:T(8,128)(2,1)}, u32[]{:S(2)}, u32[]{:S(2)}) collective-permute-start(bf16[800,800]{1,0:T(8,128)(2,1)} %shard_map.400), channel_id=1, source_target_pairs={{0,1},{1,0},{2,3},{3,2},{4,5},{5,4},{6,7},{7,6},{8,9},{9,8},{10,11... | collective-permute-start | bytes 3840008 | tf_op jit(solution)/shard_map/ppermute | solution.py:51
  463.2 4.8 %collective-permute-start.48 = (bf16[224,800]{1,0:T(8,128)(2,1)S(1)}, bf16[224,800]{1,0:T(8,128)(2,1)S(1)}, u32[]{:S(2)}, u32[]{:S(2)}) collective-permute-start(bf16[224,800]{1,0:T(8,128)(2,1)S(1)} %shard_map.399), channel_id=1, source_target_pairs={{0,1},{1,0},{2,3},{3,2},{4,5},{5,4},{6,7},{7,6},{8,9},{9,8},{10,11... | collective-permute-start | bytes 1075208 | tf_op jit(solution)/shard_map/ppermute | solution.py:51
  (104 other events, 1075.3 us)
Sparse Core Ops, SparseCore 0:
  22.4 74.9 all-gather.5
  235.5 66.3 all-gather.7
  305.4 73.5 all-gather.9

commit v2 on v1

--- a/solution.py
+++ b/solution.py
@@ -73,16 +73,57 @@
     )
 
 
-def gene_gather(values):
+def first_gather(counts_turned, share, noise):
     count = lax.axis_size("gene")
     me = lax.axis_index("gene")
-    gathered = jnp.zeros((count,) + values.shape, values.dtype)
-    for distance in range(0, count, 2):
-        near = values if distance == 0 else swap(values, distance, "gene")
-        far = swap(near, 1, "gene")
-        gathered = lax.dynamic_update_index_in_dim(gathered, near, me ^ distance, 0)
-        gathered = lax.dynamic_update_index_in_dim(gathered, far, me ^ distance ^ 1, 0)
-    return gathered.reshape((count * values.shape[0],) + values.shape[1:])
+    even = (me & 1) == 0
+    ring = [(device, (device + 2) % count) for device in range(count)]
+    steps = count // 2
+    height, width = counts_turned.shape
+    rows, depth = share.shape
+    near = jnp.concatenate([counts_turned, lengthen(share, 1, width)])
+    whole = jnp.zeros((count, height, width), counts_turned.dtype)
+    shares = jnp.zeros((count, 4, rows, depth), share.dtype)
+    at_x, at_core = {}, {}
+    distance, noise_place, noise_shape = count // 2, 0, noise.shape
+    for step in range(steps + 2):
+        moves = {}
+        if distance:
+            moves["noise"] = join(noise, distance, "gene", noise_place)
+        if step < steps:
+            moves["far"] = swap(near, 1, "gene")
+        if step < steps - 1:
+            moves["near"] = lax.ppermute(near, "gene", ring)
+        if step - 1 in at_x:
+            moves["x"] = join(at_x[step - 1], 2, "cell", 1)
+        if step - 2 in at_core:
+            moves["core"] = join(at_core[step - 2], 1, "cell", 2)
+        moves = lax.optimization_barrier(moves)
+        if distance:
+            noise = moves["noise"]
+            distance //= 2
+            noise_place += 1
+        if step < steps:
+            source = (me + count - 2 * step) % count
+            far = moves["far"]
+            whole = lax.dynamic_update_index_in_dim(whole, near[:height], source, 0)
+            whole = lax.dynamic_update_index_in_dim(whole, far[:height], source ^ 1, 0)
+            own, other = near[height:, :depth], far[height:, :depth]
+            at_x[step] = jnp.stack([jnp.where(even, own, other), jnp.where(even, other, own)])
+        if step < steps - 1:
+            near = moves["near"]
+        if "x" in moves:
+            at_core[step - 1] = moves["x"]
+        if "core" in moves:
+            base = (me + count - 2 * (step - 2)) % count - (me & 1)
+            shares = lax.dynamic_update_slice(
+                shares, moves["core"].reshape(2, 4, rows, depth), (base, 0, 0, 0)
+            )
+    return (
+        whole.reshape(count * height, width),
+        shares.reshape(-1, depth),
+        noise.reshape(count * noise_shape[0], noise_shape[1]),
+    )
 
 
 def scatter_pieces(pieces, moments):
@@ -122,23 +163,16 @@
     return values.reshape(shape[:at] + (lax.axis_size(axis),) + shape[at:])
 
 
-def cell_total(values, kind=jnp.float32):
+def cell_total(values):
     count = lax.axis_size("cell")
-    me = lax.axis_index("cell")
     distance = 1
     while distance < count:
-        half = values.shape[0] // 2
-        upper = ((me & distance) != 0).astype(jnp.int32)
-        keep = lax.dynamic_slice_in_dim(values, upper * half, half, 0)
-        give = lax.dynamic_slice_in_dim(values, (1 - upper) * half, half, 0)
-        values = keep + swap(give, distance, "cell")
+        values = halve(values, distance)
         distance *= 2
-    if kind == jnp.bfloat16:
-        values = low(lax.reduce_precision(values, 8, 7))
     while distance > 1:
         distance //= 2
-        values = join(values, distance, "cell", 0).reshape(-1, values.shape[1])
-    return values.astype(jnp.float32)
+        values = unite(values, distance)
+    return values
 
 
 def by_core(mine):
@@ -147,9 +181,28 @@
     return jnp.where(odd, other, mine), jnp.where(odd, mine, other)
 
 
-def gather_pieces(block, heights):
+def halve(values, distance, kind=jnp.float32):
+    half = values.shape[0] // 2
+    upper = ((lax.axis_index("cell") & distance) != 0).astype(jnp.int32)
+    keep = lax.dynamic_slice_in_dim(values, upper * half, half, 0)
+    give = lax.dynamic_slice_in_dim(values, (1 - upper) * half, half, 0)
+    return keep + swap(give.astype(kind), distance, "cell").astype(jnp.float32)
+
+
+def unite(values, distance):
+    return join(values, distance, "cell", 0).reshape(-1, values.shape[1])
+
+
+def rounded(values):
+    return low(lax.reduce_precision(values, 8, 7))
+
+
+def gather_block(block):
+    return lax.all_gather(block, ("gene", "cell"), axis=0, tiled=False)
+
+
+def cut_pieces(gathered, heights):
     count = lax.axis_size("cell")
-    gathered = lax.all_gather(block, ("gene", "cell"), axis=0, tiled=False)
     start = 0
     whole = []
     for height in heights:
@@ -209,68 +262,63 @@
     return (low(grad_in), sums[1], sums[0])
 
 
-def orthogonal_shared(own):
-    total = lax.psum(jnp.sum(own * own), "gene")
+def orthogonal_shared(own, axes="gene"):
+    total = lax.psum(jnp.sum(own * own), axes)
     current = own / (jnp.sqrt(total) + 1e-07)
     for iteration in range(NS):
         operand = low(current)
-        gram = lax.psum(inner_rows(operand, operand), "gene")
+        gram = lax.psum(inner_rows(operand, operand), axes)
         gram_low = low(gram)
         polynom = low(COEF_B * gram + COEF_C * rows_times(gram_low, gram_low))
         current = COEF_A * current + rows_times(operand, polynom)
     return current
 
 
-def iterate(operand, gram, gram_low, polynom, own=None, own_low=None):
-    gram[...] = outer_cols(operand[...], operand[...])
+def iterate(operand, gram, gram_low, polynom):
+    gram[...] = outer_cols(operand, operand)
     gram_low[...] = low(gram[...])
     square = rows_times(gram_low[...], gram_low[...])
     polynom[...] = low(COEF_B * gram[...] + COEF_C * square)
-    if own is not None:
-        own[...] = COEF_A * own[...] + rows_times(polynom[...], own_low[...])
-        own_low[...] = low(own[...])
-
-
-def square_kernel(place, even, odd, result, current, operand, gram, gram_low, polynom):
-    def load(moment):
-        values = moment[...]
-        current[...] = values * (1.0 / (jnp.sqrt(jnp.sum(values * values)) + 1e-07))
-
-    pl.when(place[0] == 0)(lambda: load(even))
-    pl.when(place[0] != 0)(lambda: load(odd))
+
+
+def square_kernel(middle, square, current, operand, gram, gram_low, polynom):
+    values = middle[...]
+    current[...] = values * (1.0 / (jnp.sqrt(jnp.sum(values * values)) + 1e-07))
 
     def step(iteration, carry):
         operand[...] = low(current[...])
-        iterate(operand, gram, gram_low, polynom)
+        iterate(operand[...], gram, gram_low, polynom)
         current[...] = COEF_A * current[...] + rows_times(polynom[...], operand[...])
         return carry
 
     lax.fori_loop(0, NS, step, 0)
-    result[...] = low(current[...])
+    square[...] = low(current[...])
 
 
 def tall_kernel(
-    place, even, odd, result, current, operand, own, own_low, gram, gram_low, polynom
+    place, even, odd, tall, current, operand, own, own_low, gram, gram_low, polynom
 ):
     rows = even.shape[0]
     tile = 256
 
     def load(moment):
-        def add_square(at, total):
-            values = moment[pl.ds(pl.multiple_of(at * tile, tile), tile), :].astype(jnp.float32)
+        def turn(at, total):
+            here = pl.ds(pl.multiple_of(at * tile, tile), tile)
+            values = moment[here, :].astype(jnp.float32)
+            current[:, here] = values.T
             return total + jnp.sum(values * values)
 
-        total = lax.fori_loop(0, rows // tile, add_square, jnp.float32(0))
+        total = lax.fori_loop(0, rows // tile, turn, jnp.float32(0))
         scale = 1.0 / (jnp.sqrt(total) + 1e-07)
 
-        def turn(at, carry):
+        def settle(at, carry):
             here = pl.ds(pl.multiple_of(at * tile, tile), tile)
-            values = moment[here, :].astype(jnp.float32).T * scale
+            values = current[:, here] * scale
             current[:, here] = values
             operand[:, here] = low(values)
             return carry
 
-        lax.fori_loop(0, rows // tile, turn, 0)
+        lax.fori_loop(0, rows // tile, settle, 0)
         mine = pl.ds(pl.multiple_of(place[1], 16), own.shape[1])
         own[...] = moment[mine, :].astype(jnp.float32).T * scale
         own_low[...] = low(own[...])
@@ -279,7 +327,9 @@
     pl.when(place[0] != 0)(lambda: load(odd))
 
     def step(iteration, carry):
-        iterate(operand, gram, gram_low, polynom, own, own_low)
+        iterate(operand[...], gram, gram_low, polynom)
+        own[...] = COEF_A * own[...] + rows_times(polynom[...], own_low[...])
+        own_low[...] = low(own[...])
 
         @pl.when(iteration < NS - 1)
         def _():
@@ -289,21 +339,40 @@
         return carry
 
     lax.fori_loop(0, NS, step, 0)
-    result[...] = low(own[...].T)
+    tall[...] = low(own[...].T)
+
+
+def two_parts(values):
+    first = low(values)
+    return first, low(values - first.astype(jnp.float32))
 
 
 def narrow_kernel(moments, results):
-    for number in range(moments.shape[0]):
+    count, rows = moments.shape[:2]
+
+    def halves(values):
+        return values[:rows] + values[rows:]
+
+    def quarters(values):
+        return halves(values[:, :rows] + values[:, rows:])
+
+    for number in range(count):
         values = moments[number]
-        results[number] = values / (jnp.sqrt(jnp.sum(values * values)) + 1e-07)
-    exact = dict(precision=lax.Precision.HIGHEST, preferred_element_type=jnp.float32)
+        results[number] = values * (1.0 / (jnp.sqrt(jnp.sum(values * values)) + 1e-07))
 
     def step(iteration, carry):
-        for number in range(moments.shape[0]):
+        for number in range(count):
             values = results[number]
-            gram = lax.dot_general(values, values, (((1,), (1,)), ((), ())), **exact)
-            polynom = COEF_B * gram + COEF_C * jnp.dot(gram, gram, **exact)
-            results[number] = COEF_A * values + jnp.dot(polynom, values, **exact)
+            first, second = two_parts(values)
+            stacked = jnp.concatenate([first, second], axis=0)
+            gram = quarters(outer_cols(stacked, stacked))
+            parts = two_parts(gram)
+            square = quarters(
+                rows_times(jnp.concatenate(parts, axis=0), jnp.concatenate(parts, axis=1))
+            )
+            parts = two_parts(COEF_B * gram + COEF_C * square)
+            change = halves(rows_times(jnp.concatenate(parts, axis=0), first))
+            results[number] = COEF_A * values + change + rows_times(parts[0], second)
         return carry
 
     lax.fori_loop(0, NS, step, 0)
@@ -316,20 +385,16 @@
         kernel,
         out_shape=shape,
         in_specs=[scalars if operand.dtype == jnp.int32 else space for operand in operands],
-        out_specs=space,
+        out_specs=jax.tree.map(lambda entry: space, shape),
         scratch_shapes=[pltpu.VMEM(*entry) for entry in scratch],
-        compiler_params=pltpu.CompilerParams(vmem_limit_bytes=48 * 2**20),
+        compiler_params=pltpu.CompilerParams(vmem_limit_bytes=52 * 2**20),
         cost_estimate=pl.CostEstimate(flops=flops, bytes_accessed=2**22, transcendentals=0),
     )(*operands)
 
 
-def pair_place():
-    return (lax.axis_index("cell") & 1).astype(jnp.int32)
-
-
 def orthogonal_squares(even, odd):
     width = even.shape[0]
-    mine = on_chip(
+    return on_chip(
         square_kernel,
         jax.ShapeDtypeStruct(even.shape, jnp.bfloat16),
         [
@@ -340,17 +405,14 @@
             ((width, width), jnp.bfloat16),
         ],
         6 * NS * width**3,
-        pair_place()[None],
-        even,
-        odd,
-    )
-    return by_core(mine)
+        jnp.where((lax.axis_index("cell") & 1) != 0, odd, even),
+    )
 
 
 def orthogonal_talls(even, odd, own_rows):
     rows, width = even.shape
-    start = (lax.axis_index("gene") * own_rows).astype(jnp.int32)
-    mine = on_chip(
+    place = [lax.axis_index("cell") & 1, lax.axis_index("gene") * own_rows]
+    return on_chip(
         tall_kernel,
         jax.ShapeDtypeStruct((own_rows, width), jnp.bfloat16),
         [
@@ -363,22 +425,22 @@
             ((width, width), jnp.bfloat16),
         ],
         2 * NS * width * width * (2 * rows + width),
-        jnp.stack([pair_place(), start]),
+        jnp.stack(place).astype(jnp.int32),
         even,
         odd,
     )
-    return by_core(mine)
 
 
 def orthogonal_narrow(moments):
     count, width, length = moments.shape
+    padded = lengthen(moments, 1, 128)
     return on_chip(
         narrow_kernel,
-        jax.ShapeDtypeStruct(moments.shape, jnp.float32),
+        jax.ShapeDtypeStruct(padded.shape, jnp.float32),
         [],
-        12 * NS * count * width * width * (2 * length + width),
-        moments,
-    )
+        8 * NS * count * padded.shape[1] ** 2 * (2 * length + padded.shape[1]),
+        padded,
+    )[:, :width]
 
 
 def vector_step(value, moment, square):
@@ -429,6 +491,7 @@
         and hidden_width % devices == 0
         and gene_local % (8 * cell_count) == 0
         and devices & (devices - 1) == 0
+        and cell_count == 4
     )
 
     def own_rows(values, rows=gene_local):
@@ -451,12 +514,13 @@
         def own_part(values):
             return lax.dynamic_slice_in_dim(values, cell_at * part, part, 0)
 
-        counts_turned = gene_gather(counts_turned)
-        enc_in_low = spread(spread(own_part(enc_in_low), "gene"), "cell", 1)
-        enc_in_low = enc_in_low.reshape(genes, hidden_width)
+        counts_turned, enc_in_low, all_noise = first_gather(
+            counts_turned, own_part(enc_in_low), noise
+        )
+        last_layer = own_part(last_layer)
+        counts_turned, last_layer = lax.optimization_barrier((counts_turned, last_layer))
         first = inner_rows(counts_turned, enc_in_low)
-        all_noise = spread(noise, "gene").reshape(group_rows, latent_width)
-        last_layer = gather_rows(own_part(last_layer), ("gene", "cell"))
+        last_layer = gather_rows(last_layer, ("gene", "cell"))
     else:
         first = lax.psum(inner_rows(counts_turned, enc_in_low), "gene")
         all_noise = gather_rows(noise, "gene")
@@ -505,13 +569,15 @@
     else:
         own_moment_out, moment_bias = gather_slices(pieces, moments)
     grad_a4, gain_four, shift_four = norm_back(grad_four, saved_four, norm_params, 3, cells)
-    grad_dec_mid = cell_total(inner_rows(three_low, grad_a4), jnp.bfloat16)
+    together = lax.optimization_barrier
+    half = jnp.bfloat16
+    grad_dec_mid = inner_rows(three_low, grad_a4)
     grad_three = outer_cols(grad_a4, dec_mid_low)
+    if whole:
+        grad_three, grad_dec_mid, decoder = together((grad_three, grad_dec_mid, decoder))
+        decoder = gather_block(decoder)
+        grad_dec_mid = halve(grad_dec_mid, 1, half)
     grad_a3, gain_three, shift_three = norm_back(grad_three, saved_three, norm_params, 2, cells)
-    if whole:
-        decoder, grad_a3 = lax.optimization_barrier((decoder, grad_a3))
-        moment_out, moment_bias = gather_pieces(decoder, [gene_local, cell_count])
-        own_moment_out = own_rows(moment_out)
     grad_dec_in = inner_rows(sample_low, grad_a3)
     grad_sample = outer_cols(grad_a3, dec_in_low)
     grad_mean = low(grad_sample + kl_scale * latent_mean)
@@ -522,36 +588,57 @@
     grad_pair = jnp.concatenate([grad_mean, grad_logvar], axis=1)
     latent_pair = jnp.concatenate([latent_low[0], latent_low[1]], axis=1)
     grad_narrow = jnp.concatenate([inner_rows(grad_pair, two_low), grad_dec_in])
-    grad_narrow = cell_total(lengthen(grad_narrow, 0, 8 * cell_count))
-    small = cell_sum(
-        jnp.concatenate([jnp.sum(grad_pair, axis=0, dtype=jnp.float32), loss_part[None]])
-    )
+    grad_narrow = lengthen(grad_narrow, 0, 8 * cell_count)
+    small = jnp.concatenate([jnp.sum(grad_pair, axis=0, dtype=jnp.float32), loss_part[None]])
     grad_two = outer_cols(grad_pair, latent_pair)
+    if whole:
+        grad_two, grad_narrow, grad_dec_mid = together((grad_two, grad_narrow, grad_dec_mid))
+        grad_dec_mid = rounded(halve(grad_dec_mid, 2, half))
+        grad_narrow = halve(grad_narrow, 1)
     grad_a2, gain_two, shift_two = norm_back(grad_two, saved_two, norm_params, 1, cells)
-    grad_enc_mid = cell_total(inner_rows(one_low, grad_a2), jnp.bfloat16)
+    grad_enc_mid = inner_rows(one_low, grad_a2)
     grad_one = outer_cols(grad_a2, enc_mid_low)
+    if whole:
+        grad_one, grad_enc_mid, grad_narrow, grad_dec_mid = together(
+            (grad_one, grad_enc_mid, grad_narrow, grad_dec_mid)
+        )
+        grad_dec_mid = unite(grad_dec_mid, 2)
+        grad_enc_mid = halve(grad_enc_mid, 1, half)
+        grad_narrow = halve(grad_narrow, 2)
     grad_a1, gain_one, shift_one = norm_back(grad_one, saved_one, norm_params, 0, cells)
     grad_enc_in = inner_rows(counts, grad_a1)
     if whole:
         encoder = scatter_pieces([grad_enc_in], [mom_enc_in])
-        moment_first = gather_pieces(low(encoder), [gene_local])[0]
-        new_mom_enc_in = own_rows(moment_first).astype(jnp.float32)
+        encoder, grad_enc_mid, grad_narrow, grad_dec_mid = together(
+            (rounded(encoder), grad_enc_mid, grad_narrow, grad_dec_mid)
+        )
+        encoder, decoder = together((encoder, decoder))
+        moment_first = cut_pieces(gather_block(encoder), [gene_local])[0]
+        moment_out, moment_bias = cut_pieces(decoder, [gene_local, cell_count])
+        grad_dec_mid = unite(grad_dec_mid, 1).astype(jnp.float32)
+        grad_enc_mid = rounded(halve(grad_enc_mid, 2, half))
+        grad_narrow = unite(grad_narrow, 2)
+        grad_dec_mid, grad_enc_mid, grad_narrow = together(
+            (grad_dec_mid, grad_enc_mid, grad_narrow)
+        )
+        grad_enc_mid = unite(unite(grad_enc_mid, 2), 1).astype(jnp.float32)
+        grad_narrow = unite(grad_narrow, 1)
+        own_moment_out = own_rows(moment_out)
     else:
         new_mom_enc_in = MOMENTUM * mom_enc_in + cell_sum(grad_enc_in)
-    new_mom_dec_out = own_moment_out.T
-
+        grad_enc_mid = cell_total(grad_enc_mid)
+        grad_dec_mid = cell_total(grad_dec_mid)
+        grad_narrow = cell_total(grad_narrow)
+    small = cell_sum(small)
     grad_latent_bias = small[: 2 * latent_width].reshape(2, latent_width)
     total = small[2 * latent_width]
     moment_bias = moment_bias[:, : gene_local // cell_count].reshape(gene_count, gene_local)
     new_mom_out_bias = lax.dynamic_index_in_dim(moment_bias, gene_at, 0, keepdims=False)
     new_out_bias = vector_step(out_bias, new_mom_out_bias, jnp.mean(moment_bias * moment_bias))
-
+    new_mom_dec_out = own_moment_out.T
+
+    new_mom_enc_mid = MOMENTUM * mom_enc_mid + grad_enc_mid
     new_mom_dec_mid = MOMENTUM * mom_dec_mid + grad_dec_mid
-    new_mom_enc_mid = MOMENTUM * mom_enc_mid + grad_enc_mid
-    turned_enc_mid, turned_dec_mid = orthogonal_squares(new_mom_enc_mid, new_mom_dec_mid)
-    new_enc_mid = enc_mid - RATE * turned_enc_mid.astype(jnp.float32)
-    new_dec_mid = dec_mid - RATE * turned_dec_mid.astype(jnp.float32)
-
     grad_latent = grad_narrow[: 2 * latent_width].reshape(2, latent_width, hidden_width)
     grad_dec_in = grad_narrow[2 * latent_width : 3 * latent_width]
     new_mom_dec_in = MOMENTUM * mom_dec_in + grad_dec_in
@@ -561,12 +648,43 @@
     factor = math.sqrt(max(1.0, hidden_width / latent_width))
     new_dec_in = dec_in - RATE * factor * narrow[2]
     new_latent_w = latent_w - RATE * jnp.swapaxes(narrow[:2], 1, 2)
-
     if whole:
-        turned_in, turned_out = orthogonal_talls(moment_first, moment_out, gene_local)
+        square = orthogonal_squares(new_mom_enc_mid, new_mom_dec_mid)
+        turned_enc_mid, turned_dec_mid = by_core(square)
+        new_enc_mid = enc_mid - RATE * turned_enc_mid.astype(jnp.float32)
+        new_dec_mid = dec_mid - RATE * turned_dec_mid.astype(jnp.float32)
+        (
+            moment_first,
+            moment_out,
+            new_mom_enc_mid,
+            new_mom_dec_mid,
+            new_mom_dec_out,
+            new_mom_latent_w,
+            new_dec_in,
+            new_latent_w,
+            new_enc_mid,
+            new_dec_mid,
+        ) = together(
+            (
+                moment_first,
+                moment_out,
+                new_mom_enc_mid,
+                new_mom_dec_mid,
+                new_mom_dec_out,
+                new_mom_latent_w,
+                new_dec_in,
+                new_latent_w,
+                new_enc_mid,
+                new_dec_mid,
+            )
+        )
+        new_mom_enc_in = own_rows(moment_first).astype(jnp.float32)
+        turned_in, turned_out = by_core(orthogonal_talls(moment_first, moment_out, gene_local))
     else:
         turned_in = orthogonal_shared(new_mom_enc_in)
         turned_out = orthogonal_shared(own_moment_out)
+        new_enc_mid = enc_mid - RATE * orthogonal_shared(new_mom_enc_mid, ())
+        new_dec_mid = dec_mid - RATE * orthogonal_shared(new_mom_dec_mid, ())
     new_enc_in = enc_in - RATE * turned_in.astype(jnp.float32)
     factor = math.sqrt(max(1.0, genes / hidden_width))
     new_dec_out = dec_out - RATE * factor * turned_out.astype(jnp.float32).T

time: 486 us -> 479 us (0.986)
  other arithmetic: 55.8 us -> 89.9 us
  waiting for transfers between devices: 146 us -> 130 us
  matrix products: 58.9 us -> 46.4 us
  Pallas kernels: 104 us -> 91.6 us
    ppermute x62, waiting for transfers between devices: 146 us -> 109 us  [swap(): return lax.ppermute(values, axis, pairs)]
    all_gather x1, waiting for transfers between devices: 0.02 us -> 21 us  [gather_rows(): return lax.all_gather(values, axes, axis=0, tiled=True)]
    reduce_sum x0 -> x3, other arithmetic: none -> 15 us  [norm_back(): jnp.sum(grad_shift, axis=0)]
    pallas_call x3, Pallas kernels: 104 us -> 91.6 us  [on_chip(): pl.pallas_call(kernel, out_shape=shape, in_specs=[scalars if operand.dtyp...]
    dot_general x5, matrix products: 21.9 us -> 14.2 us  [outer_cols(): lax.dot_general(left, right, (((1,), (1,)), ((), ())), preferred_element_...]
    ppermute x62, starting transfers between devices: 51.7 us -> 46.7 us  [swap(): return lax.ppermute(values, axis, pairs)]
    unnamed x210 -> x202, local copies, waits for them, and re-layouts: 8.44 us -> 10.8 us
  transfers between devices with their start and end apart: 65 -> 68, of which waited for: 29 -> 26; matrix products, arithmetic and copies ran while one was open for 20% -> 29% of each run, Pallas kernels for 11% -> 9%
where the time goes in v2:
time: 479 us; the launch traced here: 470 us
  waiting for transfers between devices  130 us (27%)
  Pallas kernels  91.6 us (19%)
  other arithmetic  89.9 us (19%)
  starting transfers between devices  48.6 us (10%)
  matrix products  46.4 us (10%)
  local copies, waits for them, and re-layouts  44.2 us (9%)
  between operations  19.9 us (4%)
    ppermute x62, waiting for transfers between devices, swap(): return lax.ppermute(values, axis, pairs)  109 us
    pallas_call x3, Pallas kernels, on_chip(): pl.pallas_call(kernel, out_shape=shape, in_specs=[scalars if operand.dtyp...  91.6 us
    ppermute x62, starting transfers between devices, swap(): return lax.ppermute(values, axis, pairs)  46.7 us
    all_gather x1, waiting for transfers between devices, gather_rows(): return lax.all_gather(values, axes, axis=0, tiled=True)  21 us
    dot_general x7, matrix products, inner_rows(): lax.dot_general(left, right, (((0,), (0,)), ((), ())), preferred_element_...  19.4 us
    convert_element_type x11, other arithmetic, low(): return values.astype(jnp.bfloat16)  19.1 us
    reduce_sum x3, other arithmetic, norm_back(): jnp.sum(grad_shift, axis=0)  15 us
    dot_general x5, matrix products, outer_cols(): lax.dot_general(left, right, (((1,), (1,)), ((), ())), preferred_element_...  14.2 us
  transfers between devices with their start and end apart: 68, of which 26 were waited for; matrix products, arithmetic and copies ran while one was open for 29% of the time, Pallas kernels for 9%

profile of v2, /device:TPU:0, one launch (start us, length us, event | category | flops | bytes accessed | tf_op | source)
XLA Modules:
  0.0 470.3 jit_solution(7853648709707174618)
XLA Ops:
  8.4 1.9 fusion.75
  10.3 3.0 collective-permute-start
  14.8 2.6 collective-permute-start.2
  22.9 1.6 slice_reduce_fusion.1
  29.2 1.8 copy-done.18
  36.9 1.8 bitcast_dynamic-update-slice_fusion.7
  38.7 1.8 bitcast_dynamic-update-slice_fusion.6
  40.5 12.0 %collective-permute-done.5 = f32[2,128,100]{1,2,0:T(8,128)S(1)} collective-permute-done((f32[2,128,100]{1,2,0:T(8,128)S(1)}, f32[2,128,100]{1,2,0:T(8,128)S(1)}, u32[]{:S(2)}, u32[]{:S(2)}) %collective-permute-start.5) | collective-permute-done | bytes 102432 | tf_op jit(solution)/shard_map/ppermute | solution.py:51
  58.3 3.6 collective-permute-done.11
  62.1 10.2 %collective-permute-done.10 = f32[2,2,128,100]{2,3,0,1:T(8,128)S(1)} collective-permute-done((f32[2,2,128,100]{2,3,0,1:T(8,128)S(1)}, f32[2,2,128,100]{2,3,0,1:T(8,128)S(1)}, u32[]{:S(2)}, u32[]{:S(2)}) %collective-permute-start.10) | collective-permute-done | bytes 204832 | tf_op jit(solution)/shard_map/ppermute | solution.py:51
  75.1 4.3 collective-permute-done.14
  79.8 9.1 %collective-permute-done.13 = bf16[280,1024]{1,0:T(8,128)(2,1)S(1)} collective-permute-done((bf16[280,1024]{1,0:T(8,128)(2,1)S(1)}, bf16[280,1024]{1,0:T(8,128)(2,1)S(1)}, u32[]{:S(2)}, u32[]{:S(2)}) %collective-permute-start.13) | collective-permute-done | bytes 573472 | tf_op jit(solution)/shard_map/ppermute | solution.py:51
  89.0 2.0 collective-permute-start.16
  91.5 4.4 collective-permute-done.16
  98.4 3.6 fusion.123
  102.2 1.8 collective-permute-start.19
  104.7 2.1 copy.65
  106.8 2.1 reshape.190
  109.8 1.8 fusion.31
  111.6 2.2 fusion.122
  114.4 1.8 collective-permute-start.22
  120.0 1.8 fusion.39
  122.4 1.9 subtract_reduce_fusion
  130.8 1.8 fusion.47
  132.8 2.2 fusion.120
  141.0 2.2 fusion.55
  145.8 21.0 %all-gather.6.cloned.1.call-done = bf16[1792,811]{1,0:T(8,128)(2,1)} async-done(((bf16[56,811]{1,0:T(8,128)(2,1)}), bf16[1792,811]{1,0:T(8,128)(2,1)}) %all-gather.6.cloned.1.call-update) | async-done | bytes 2906640 | tf_op jit(solution)/shard_map/all_gather | solution.py:236
  168.2 2.3 fusion.76
  171.9 5.9 %multiply_convert_fusion = (bf16[1792,1024]{1,0:T(8,128)(2,1)S(1)}, f32[]{:T(128)}) fusion(f32[1792,1024]{1,0:T(8,128)S(1)} %fusion.76, bf16[1792,1024]{1,0:T(8,128)(2,1)S(1)} %bitcast.248, f32[1792]{0:T(1024)S(1)} %convert_reduce_fusion.1, bf16[1024,800]{0,1:T(8,128)(2,1)S(1)} %copy-done.9, bf16[1792,811]{1,0:T(8,128)(2,1)S(1)} %copy-done.51), kind=kOutput, calls=%fused_computation.1 | convolution fusion | flops 2950692864 | bytes 19232260 | tf_op jit(solution)/shard_map/dot_general | solution.py:30
  177.8 1.6 fusion.78
  180.2 7.5 %fusion.119 = (f32[800]{0:T(1024)S(1)}, f32[800]{0:T(1024)S(1)}, f32[1024,800]{0,1:T(8,128)}) fusion(f32[800]{0:T(1024)S(1)} %add_rsqrt_fusion.2, f32[1024,800]{0,1:T(8,128)S(1)} %copy-done.7, f32[800]{0:T(1024)S(1)} %get-tuple-element.104, f32[800]{0:T(1024)S(1)} %copy-done.78, f32[800]{0:T(1024)S(1)} %copy-done.70, ...), kind=kOutput, calls=%fused_computation.366 | convolution fusion | flops 2957310464 | bytes 13149440 | tf_op jit(solution)/shard_map/dot_general | solution.py:24
  199.8 3.9 multiply_convert_fusion.4
  203.7 3.5 fusion.67
  207.3 3.5 fusion.127
  210.8 1.9 fusion.89
  212.7 6.4 %fusion.118 = (f32[800]{0:T(1024)S(1)}, f32[800]{0:T(1024)S(1)}, f32[1024,800]{0,1:T(8,128)}) fusion(f32[800]{0:T(1024)S(1)} %add_rsqrt_fusion.3, f32[1024,800]{0,1:T(8,128)S(1)} %get-tuple-element.106, f32[800]{0:T(1024)S(1)} %get-tuple-element.107, f32[1024,800]{0,1:T(8,128)} %fusion.67, f32[800]{0:T(1024)S(1)} %copy-done.68, f32[800]{0:T(1024)S(1)} %copy-done.61), kind=kLoop, calls=%fused_computation.365 | loop fusion | flops 21297600 | bytes 9849600 | tf_op jit(solution)/shard_map/reduce_sum | solution.py:258
  221.4 2.3 dynamic-slice_convert_fusion.1
  225.4 2.7 multiply_convert_fusion.3
  232.3 2.3 fusion.82
  236.1 1.7 convert_add_fusion.2
  237.8 5.3 %fusion.117 = (f32[800]{0:T(1024)S(1)}, f32[800]{0:T(1024)S(1)}, f32[1024,800]{0,1:T(8,128)S(1)}) fusion(f32[800]{0:T(1024)S(1)} %add_rsqrt_fusion, f32[1024,800]{0,1:T(8,128)S(1)} %copy-done.3, f32[800]{0:T(1024)S(1)} %get-tuple-element.113, f32[1024,800]{0,1:T(8,128)} %fusion.82, f32[800]{0:T(1024)S(1)} %copy-done.66, f32[800]{0:T(1024)S(1)} %copy-done.60), kind=kLoop, calls=%fused_computation.364 | loop fusion | flops 21297600 | bytes 9849600 | tf_op jit(solution)/shard_map/reduce_sum | solution.py:258
  249.9 1.9 fusion.71
  251.8 1.9 fusion.129
  253.7 7.2 %collective-permute-done.47 = bf16[200,800]{1,0:T(8,128)(2,1)S(1)} collective-permute-done((bf16[200,800]{1,0:T(8,128)(2,1)S(1)}, bf16[200,800]{1,0:T(8,128)(2,1)S(1)}, u32[]{:S(2)}, u32[]{:S(2)}) %collective-permute-start.47) | collective-permute-done | bytes 320032 | tf_op jit(solution)/shard_map/ppermute | solution.py:51
  261.8 3.3 fusion.116
  265.3 2.2 collective-permute-start.49
  267.6 1.7 collective-permute-start.56
  276.5 15.2 %collective-permute-done.52 = f32[56,800]{1,0:T(8,128)S(1)} collective-permute-done((f32[56,800]{1,0:T(8,128)S(1)}, f32[56,800]{1,0:T(8,128)S(1)}, u32[]{:S(2)}, u32[]{:S(2)}) %collective-permute-start.52) | collective-permute-done | bytes 179232 | tf_op jit(solution)/shard_map/ppermute | solution.py:51
  291.7 8.3 %collective-permute-done.53 = f32[56,800]{1,0:T(8,128)S(1)} collective-permute-done((f32[56,800]{1,0:T(8,128)S(1)}, f32[56,800]{1,0:T(8,128)S(1)}, u32[]{:S(2)}, u32[]{:S(2)}) %collective-permute-start.53) | collective-permute-done | bytes 179232 | tf_op jit(solution)/shard_map/ppermute | solution.py:51
  300.0 1.6 fusion.92
  301.6 4.9 %collective-permute-done.55 = f32[80,800]{1,0:T(8,128)} collective-permute-done((f32[80,800]{1,0:T(8,128)}, f32[80,800]{1,0:T(8,128)}, u32[]{:S(2)}, u32[]{:S(2)}) %collective-permute-start.55) | collective-permute-done | bytes 256032 | tf_op jit(solution)/shard_map/ppermute | solution.py:51
  310.1 1.8 collective-permute-start.59
  314.3 5.6 %collective-permute-done.59 = f32[80,800]{1,0:T(8,128)S(1)} collective-permute-done((f32[80,800]{1,0:T(8,128)S(1)}, f32[80,800]{1,0:T(8,128)S(1)}, u32[]{:S(2)}, u32[]{:S(2)}) %collective-permute-start.59) | collective-permute-done | bytes 256032 | tf_op jit(solution)/shard_map/ppermute | solution.py:51
  320.0 6.3 %collective-permute-done.58 = bf16[200,800]{1,0:T(8,128)(2,1)S(1)} collective-permute-done((bf16[200,800]{1,0:T(8,128)(2,1)S(1)}, bf16[200,800]{1,0:T(8,128)(2,1)S(1)}, u32[]{:S(2)}, u32[]{:S(2)}) %collective-permute-start.58) | collective-permute-done | bytes 320032 | tf_op jit(solution)/shard_map/ppermute | solution.py:51
  328.8 7.4 %collective-permute-done.60 = bf16[200,800]{1,0:T(8,128)(2,1)S(1)} collective-permute-done((bf16[200,800]{1,0:T(8,128)(2,1)S(1)}, bf16[200,800]{1,0:T(8,128)(2,1)S(1)}, u32[]{:S(2)}, u32[]{:S(2)}) %collective-permute-start.60) | collective-permute-done | bytes 320032 | tf_op jit(solution)/shard_map/ppermute | solution.py:51
  339.7 1.7 select_bitcast_fusion.1
  342.3 3.9 broadcast_select_fusion
  346.2 29.1 %shard_map.400 = bf16[800,800]{1,0:T(8,128)(2,1)S(1)} custom-call(f32[800,800]{1,0:T(8,128)} %get-tuple-element.230.middle), custom_call_target="tpu_custom_call" | custom-call | flops 15360000000 | bytes 4194304 | tf_op jit(solution)/shard_map/pallas_call | solution.py:384
  378.6 13.2 %shard_map.399 = f32[3,128,800]{2,1,0:T(8,128)S(1)} custom-call(f32[3,128,800]{2,1,0:T(8,128)} %select_maximum_fusion.moments), custom_call_target="tpu_custom_call" | custom-call | flops 3397386240 | bytes 4194304 | tf_op jit(solution)/shard_map/pallas_call | solution.py:384
  393.9 5.4 %multiply_subtract_fusion = (f32[800,800]{1,0:T(8,128)}, f32[800,800]{1,0:T(8,128)}) fusion(f32[800,800]{1,0:T(8,128)S(1)} %copy-done.35, bf16[800,800]{1,0:T(8,128)(2,1)S(1)} %shard_map.400, bf16[800,800]{1,0:T(8,128)(2,1)} %collective-permute-done.63, pred[]{:T(512)S(6)} %ne.68, f32[800,800]{1,0:T(8,128)S(1)} %copy-done.32), kind=kLoop, calls=%fused_computation.88 | loop fusion | flops 5120000 | bytes 12800001 | tf_op jit(solution)/shard_map/sub | solution.py:655
  399.3 3.2 slice.234
  403.2 2.1 dynamic-slice_bitcast_fusion
  405.2 49.3 %shard_map.401 = bf16[224,800]{1,0:T(8,128)(2,1)S(1)} custom-call(s32[2]{0:T(128)S(1)} %pad_add_fusion.place, bf16[1792,800]{1,0:T(8,128)(2,1)} %all-gather.10.cloned.1.call-done.even, f32[1792,800]{1,0:T(8,128)} %bitcast.238), custom_call_target="tpu_custom_call" | custom-call | flops 28057600000 | bytes 4194304 | tf_op jit(solution)/shard_map/pallas_call | solution.py:384
  458.4 1.9 dynamic-slice_convert_fusion.4
  (498 shorter events, 114.1 us)
Async XLA Ops:
  7.2 159.6 %all-gather.6.cloned.1.call-start = ((), (), s32[]{:S(2)}) async-start(), calls=%async_computation | async-start | bytes 3311616 | tf_op jit(solution)/shard_map/all_gather | solution.py:236
  10.3 22.7 %collective-permute-start = (bf16[280,1024]{1,0:T(8,128)(2,1)}, bf16[280,1024]{1,0:T(8,128)(2,1)}, u32[]{:S(2)}, u32[]{:S(2)}) collective-permute-start(bf16[280,1024]{1,0:T(8,128)(2,1)} %fusion.75), channel_id=1, source_target_pairs={{0,4},{4,0},{8,12},{12,8},{16,20},{20,16},{24,28},{28,24},{1,5},{5... | collective-permute-start | bytes 1720328 | tf_op jit(solution)/shard_map/ppermute | solution.py:51
  13.2 19.8 %collective-permute-start.1 = (bf16[280,1024]{1,0:T(8,128)(2,1)}, bf16[280,1024]{1,0:T(8,128)(2,1)}, u32[]{:S(2)}, u32[]{:S(2)}) collective-permute-start(bf16[280,1024]{1,0:T(8,128)(2,1)} %fusion.75), channel_id=1, source_target_pairs={{0,8},{4,12},{8,16},{12,20},{16,24},{20,28},{24,0},{28,4},{1,9},{5... | collective-permute-start | bytes 1720328 | tf_op jit(solution)/shard_map/ppermute | solution.py:96
  14.8 17.3 %collective-permute-start.2 = (f32[128,100]{0,1:T(8,128)}, f32[128,100]{0,1:T(8,128)}, u32[]{:S(2)}, u32[]{:S(2)}) collective-permute-start(f32[128,100]{0,1:T(8,128)} %param.27), channel_id=1, source_target_pairs={{0,16},{4,20},{8,24},{12,28},{16,0},{20,4},{24,8},{28,12},{1,17},{... | collective-permute-start | bytes 153608 | tf_op jit(solution)/shard_map/ppermute | solution.py:51
  33.0 19.7 %collective-permute-start.3 = (bf16[280,1024]{1,0:T(8,128)(2,1)}, bf16[280,1024]{1,0:T(8,128)(2,1)S(1)}, u32[]{:S(2)}, u32[]{:S(2)}) collective-permute-start(bf16[280,1024]{1,0:T(8,128)(2,1)} %collective-permute-done.1), channel_id=1, source_target_pairs={{0,4},{4,0},{8,12},{12,8},{16,20},{20,16},{24,28},{28,24},{1,5},{5... | collective-permute-start | bytes 1720328 | tf_op jit(solution)/shard_map/ppermute | solution.py:51
  33.6 19.1 %collective-permute-start.4 = (bf16[280,1024]{1,0:T(8,128)(2,1)}, bf16[280,1024]{1,0:T(8,128)(2,1)S(1)}, u32[]{:S(2)}, u32[]{:S(2)}) collective-permute-start(bf16[280,1024]{1,0:T(8,128)(2,1)} %collective-permute-done.1), channel_id=1, source_target_pairs={{0,8},{4,12},{8,16},{12,20},{16,24},{20,28},{24,0},{28,4},{1,9},{5... | collective-permute-start | bytes 1720328 | tf_op jit(solution)/shard_map/ppermute | solution.py:96
  34.6 17.9 %collective-permute-start.6 = (bf16[2,56,800]{2,1,0:T(8,128)(2,1)S(1)}, bf16[2,56,800]{2,1,0:T(8,128)(2,1)S(1)}, u32[]{:S(2)}, u32[]{:S(2)}) collective-permute-start(bf16[2,56,800]{2,1,0:T(8,128)(2,1)S(1)} %pad_maximum_fusion.17), channel_id=1, source_target_pairs={{0,2},{1,3},{2,0},{3,1},{4,6},{5,7},{6,4},{7,5},{8,10},{9,11},{10,... | collective-permute-start | bytes 537608 | tf_op jit(solution)/shard_map/ppermute | solution.py:51
  36.2 16.3 %collective-permute-start.5 = (f32[2,128,100]{1,2,0:T(8,128)S(1)}, f32[2,128,100]{1,2,0:T(8,128)S(1)}, u32[]{:S(2)}, u32[]{:S(2)}) collective-permute-start(f32[2,128,100]{1,2,0:T(8,128)S(1)} %pad_maximum_fusion.21), channel_id=1, source_target_pairs={{0,8},{4,12},{8,0},{12,4},{16,24},{20,28},{24,16},{28,20},{1,9},{5... | collective-permute-start | bytes 307208 | tf_op jit(solution)/shard_map/ppermute | solution.py:51
  52.7 20.6 %collective-permute-start.8 = (bf16[280,1024]{1,0:T(8,128)(2,1)S(1)}, bf16[280,1024]{1,0:T(8,128)(2,1)S(1)}, u32[]{:S(2)}, u32[]{:S(2)}) collective-permute-start(bf16[280,1024]{1,0:T(8,128)(2,1)S(1)} %collective-permute-done.4), channel_id=1, source_target_pairs={{0,4},{4,0},{8,12},{12,8},{16,20},{20,16},{24,28},{28,24},{1,5},{5... | collective-permute-start | bytes 1720328 | tf_op jit(solution)/shard_map/ppermute | solution.py:51
  54.3 19.0 %collective-permute-start.9 = (bf16[280,1024]{1,0:T(8,128)(2,1)S(1)}, bf16[280,1024]{1,0:T(8,128)(2,1)S(1)}, u32[]{:S(2)}, u32[]{:S(2)}) collective-permute-start(bf16[280,1024]{1,0:T(8,128)(2,1)S(1)} %collective-permute-done.4), channel_id=1, source_target_pairs={{0,8},{4,12},{8,16},{12,20},{16,24},{20,28},{24,0},{28,4},{1,9},{5... | collective-permute-start | bytes 1720328 | tf_op jit(solution)/shard_map/ppermute | solution.py:96
  55.2 6.7 %collective-permute-start.11 = (bf16[2,56,800]{2,1,0:T(8,128)(2,1)S(1)}, bf16[2,56,800]{2,1,0:T(8,128)(2,1)S(1)}, u32[]{:S(2)}, u32[]{:S(2)}) collective-permute-start(bf16[2,56,800]{2,1,0:T(8,128)(2,1)S(1)} %pad_maximum_fusion.18), channel_id=1, source_target_pairs={{0,2},{1,3},{2,0},{3,1},{4,6},{5,7},{6,4},{7,5},{8,10},{9,11},{10,... | collective-permute-start | bytes 537608 | tf_op jit(solution)/shard_map/ppermute | solution.py:51
  56.2 16.1 %collective-permute-start.10 = (f32[2,2,128,100]{2,3,0,1:T(8,128)S(1)}, f32[2,2,128,100]{2,3,0,1:T(8,128)S(1)}, u32[]{:S(2)}, u32[]{:S(2)}) collective-permute-start(f32[2,2,128,100]{2,3,0,1:T(8,128)S(1)} %pad_maximum_fusion.16), channel_id=1, source_target_pairs={{0,4},{4,0},{8,12},{12,8},{16,20},{20,16},{24,28},{28,24},{1,5},{5... | collective-permute-start | bytes 614408 | tf_op jit(solution)/shard_map/ppermute | solution.py:51
  56.7 16.4 %collective-permute-start.7 = (bf16[2,2,56,800]{3,2,1,0:T(8,128)(2,1)S(1)}, bf16[2,2,56,800]{3,2,1,0:T(8,128)(2,1)S(1)}, u32[]{:S(2)}, u32[]{:S(2)}) collective-permute-start(bf16[2,2,56,800]{3,2,1,0:T(8,128)(2,1)S(1)} %pad_maximum_fusion.12), channel_id=1, source_target_pairs={{0,1},{1,0},{2,3},{3,2},{4,5},{5,4},{6,7},{7,6},{8,9},{9,8},{10,11... | collective-permute-start | bytes 1075208 | tf_op jit(solution)/shard_map/ppermute | solution.py:51
  73.4 6.1 %collective-permute-start.14 = (bf16[2,56,800]{2,1,0:T(8,128)(2,1)S(1)}, bf16[2,56,800]{2,1,0:T(8,128)(2,1)S(1)}, u32[]{:S(2)}, u32[]{:S(2)}) collective-permute-start(bf16[2,56,800]{2,1,0:T(8,128)(2,1)S(1)} %pad_maximum_fusion.19), channel_id=1, source_target_pairs={{0,2},{1,3},{2,0},{3,1},{4,6},{5,7},{6,4},{7,5},{8,10},{9,11},{10,... | collective-permute-start | bytes 537608 | tf_op jit(solution)/shard_map/ppermute | solution.py:51
  73.4 6.2 %collective-permute-start.12 = (bf16[2,2,56,800]{3,2,0,1:T(8,128)(2,1)S(1)}, bf16[2,2,56,800]{3,2,0,1:T(8,128)(2,1)S(1)}, u32[]{:S(2)}, u32[]{:S(2)}) collective-permute-start(bf16[2,2,56,800]{3,2,0,1:T(8,128)(2,1)S(1)} %pad_maximum_fusion.13), channel_id=1, source_target_pairs={{0,1},{1,0},{2,3},{3,2},{4,5},{5,4},{6,7},{7,6},{8,9},{9,8},{10,11... | collective-permute-start | bytes 1075208 | tf_op jit(solution)/shard_map/ppermute | solution.py:51
  73.5 15.4 %collective-permute-start.13 = (bf16[280,1024]{1,0:T(8,128)(2,1)S(1)}, bf16[280,1024]{1,0:T(8,128)(2,1)S(1)}, u32[]{:S(2)}, u32[]{:S(2)}) collective-permute-start(bf16[280,1024]{1,0:T(8,128)(2,1)S(1)} %collective-permute-done.9), channel_id=1, source_target_pairs={{0,4},{4,0},{8,12},{12,8},{16,20},{20,16},{24,28},{28,24},{1,5},{5... | collective-permute-start | bytes 1720328 | tf_op jit(solution)/shard_map/ppermute | solution.py:51
  89.0 6.9 %collective-permute-start.16 = (bf16[2,56,800]{2,1,0:T(8,128)(2,1)S(1)}, bf16[2,56,800]{2,1,0:T(8,128)(2,1)S(1)}, u32[]{:S(2)}, u32[]{:S(2)}) collective-permute-start(bf16[2,56,800]{2,1,0:T(8,128)(2,1)S(1)} %pad_maximum_fusion.20), channel_id=1, source_target_pairs={{0,2},{1,3},{2,0},{3,1},{4,6},{5,7},{6,4},{7,5},{8,10},{9,11},{10,... | collective-permute-start | bytes 537608 | tf_op jit(solution)/shard_map/ppermute | solution.py:51
  91.4 4.6 collective-permute-start.15
  102.0 7.1 %collective-permute-start.18 = (f32[2,800]{1,0:T(2,128)S(1)}, f32[2,800]{1,0:T(2,128)S(1)}, u32[]{:S(2)}, u32[]{:S(2)}) collective-permute-start(f32[2,800]{1,0:T(2,128)S(1)} %pad_maximum_fusion.24), channel_id=1, source_target_pairs={{0,1},{1,0},{2,3},{3,2},{4,5},{5,4},{6,7},{7,6},{8,9},{9,8},{10,11... | collective-permute-start | bytes 19208 | tf_op jit(solution)/shard_map/ppermute | solution.py:51
  102.2 6.9 %collective-permute-start.19 = (f32[2,800]{1,0:T(2,128)S(1)}, f32[2,800]{1,0:T(2,128)S(1)}, u32[]{:S(2)}, u32[]{:S(2)}) collective-permute-start(f32[2,800]{1,0:T(2,128)S(1)} %pad_maximum_fusion.24), channel_id=1, source_target_pairs={{0,2},{1,3},{2,0},{3,1},{4,6},{5,7},{6,4},{7,5},{8,10},{9,11},{10,... | collective-permute-start | bytes 19208 | tf_op jit(solution)/shard_map/ppermute | solution.py:51
  104.0 5.1 %collective-permute-start.20 = (f32[2,800]{1,0:T(2,128)S(1)}, f32[2,800]{1,0:T(2,128)S(1)}, u32[]{:S(2)}, u32[]{:S(2)}) collective-permute-start(f32[2,800]{1,0:T(2,128)S(1)} %pad_maximum_fusion.24), channel_id=1, source_target_pairs={{0,3},{1,2},{2,1},{3,0},{4,7},{5,6},{6,5},{7,4},{8,11},{9,10},{10,... | collective-permute-start | bytes 19208 | tf_op jit(solution)/shard_map/ppermute | solution.py:51
  108.9 228.3 %all-gather.8.cloned.1.call-start = ((), (), s32[]{:S(2)}) async-start(), calls=%async_computation.1 | async-start | bytes 7569408 | tf_op jit(solution)/shard_map/all_gather | solution.py:201
  114.4 3.6 collective-permute-start.22
  116.1 3.3 collective-permute-start.23
  125.7 3.1 collective-permute-start.24
  125.9 4.0 collective-permute-start.25
  126.6 3.4 collective-permute-start.26
  135.3 3.6 collective-permute-start.28
  136.6 3.1 collective-permute-start.29
  188.9 9.4 %collective-permute-start.30 = (f32[2,800]{1,0:T(2,128)}, f32[2,800]{1,0:T(2,128)}, u32[]{:S(2)}, u32[]{:S(2)}) collective-permute-start(f32[2,800]{1,0:T(2,128)} %pad_maximum_fusion.28), channel_id=1, source_target_pairs={{0,1},{1,0},{2,3},{3,2},{4,5},{5,4},{6,7},{7,6},{8,9},{9,8},{10,11... | collective-permute-start | bytes 19208 | tf_op jit(solution)/shard_map/ppermute | solution.py:51
  189.1 9.3 %collective-permute-start.31 = (f32[2,800]{1,0:T(2,128)}, f32[2,800]{1,0:T(2,128)}, u32[]{:S(2)}, u32[]{:S(2)}) collective-permute-start(f32[2,800]{1,0:T(2,128)} %pad_maximum_fusion.28), channel_id=1, source_target_pairs={{0,2},{1,3},{2,0},{3,1},{4,6},{5,7},{6,4},{7,5},{8,10},{9,11},{10,... | collective-permute-start | bytes 19208 | tf_op jit(solution)/shard_map/ppermute | solution.py:51
  190.4 8.1 %collective-permute-start.32 = (f32[2,800]{1,0:T(2,128)}, f32[2,800]{1,0:T(2,128)}, u32[]{:S(2)}, u32[]{:S(2)}) collective-permute-start(f32[2,800]{1,0:T(2,128)} %pad_maximum_fusion.28), channel_id=1, source_target_pairs={{0,3},{1,2},{2,1},{3,0},{4,7},{5,6},{6,5},{7,4},{8,11},{9,10},{10,... | collective-permute-start | bytes 19208 | tf_op jit(solution)/shard_map/ppermute | solution.py:51
  195.8 14.9 %collective-permute-start.33 = (f32[64,800]{1,0:T(8,128)}, f32[64,800]{1,0:T(8,128)}, u32[]{:S(2)}, u32[]{:S(2)}) collective-permute-start(f32[64,800]{1,0:T(8,128)} %get-tuple-element.262), channel_id=1, source_target_pairs={{0,1},{1,0},{2,3},{3,2},{4,5},{5,4},{6,7},{7,6},{8,9},{9,8},{10,11... | collective-permute-start | bytes 614408 | tf_op jit(solution)/shard_map/ppermute | solution.py:51
  196.4 14.4 %collective-permute-start.34 = (f32[64,800]{1,0:T(8,128)}, f32[64,800]{1,0:T(8,128)}, u32[]{:S(2)}, u32[]{:S(2)}) collective-permute-start(f32[64,800]{1,0:T(8,128)} %get-tuple-element.261), channel_id=1, source_target_pairs={{0,2},{1,3},{2,0},{3,1},{4,6},{5,7},{6,4},{7,5},{8,10},{9,11},{10,... | collective-permute-start | bytes 614408 | tf_op jit(solution)/shard_map/ppermute | solution.py:51
  198.3 12.5 %collective-permute-start.35 = (f32[64,800]{1,0:T(8,128)}, f32[64,800]{1,0:T(8,128)S(1)}, u32[]{:S(2)}, u32[]{:S(2)}) collective-permute-start(f32[64,800]{1,0:T(8,128)} %get-tuple-element.260), channel_id=1, source_target_pairs={{0,3},{1,2},{2,1},{3,0},{4,7},{5,6},{6,5},{7,4},{8,11},{9,10},{10,... | collective-permute-start | bytes 614408 | tf_op jit(solution)/shard_map/ppermute | solution.py:51
  219.2 5.4 %collective-permute-start.36 = (f32[2,800]{1,0:T(2,128)S(1)}, f32[2,800]{1,0:T(2,128)S(1)}, u32[]{:S(2)}, u32[]{:S(2)}) collective-permute-start(f32[2,800]{1,0:T(2,128)S(1)} %pad_maximum_fusion.29), channel_id=1, source_target_pairs={{0,1},{1,0},{2,3},{3,2},{4,5},{5,4},{6,7},{7,6},{8,9},{9,8},{10,11... | collective-permute-start | bytes 19208 | tf_op jit(solution)/shard_map/ppermute | solution.py:51
  220.0 4.5 collective-permute-start.37
  221.3 3.3 collective-permute-start.38
  223.7 12.3 %collective-permute-start.42 = (bf16[400,800]{1,0:T(8,128)(2,1)}, bf16[400,800]{1,0:T(8,128)(2,1)}, u32[]{:S(2)}, u32[]{:S(2)}) collective-permute-start(bf16[400,800]{1,0:T(8,128)(2,1)} %dynamic-slice_convert_fusion.1), channel_id=1, source_target_pairs={{0,1},{1,0},{2,3},{3,2},{4,5},{5,4},{6,7},{7,6},{8,9},{9,8},{10,11... | collective-permute-start | bytes 1920008 | tf_op jit(solution)/shard_map/ppermute | solution.py:51
  224.5 180.8 %all-gather.10.cloned.1.call-start = ((), (), s32[]{:S(2)}) async-start(), calls=%async_computation.2 | async-start | bytes 3311616 | tf_op jit(solution)/shard_map/all_gather | solution.py:201
  229.0 6.8 %collective-permute-start.39 = (f32[201]{0:T(256)S(1)}, f32[201]{0:T(256)S(1)}, u32[]{:S(2)}, u32[]{:S(2)}) collective-permute-start(f32[201]{0:T(256)S(1)} %pad_maximum_fusion.32), channel_id=1, source_target_pairs={{0,1},{1,0},{2,3},{3,2},{4,5},{5,4},{6,7},{7,6},{8,9},{9,8},{10,11... | collective-permute-start | bytes 2420 | tf_op jit(solution)/shard_map/ppermute | solution.py:51
  229.0 6.7 %collective-permute-start.40 = (f32[201]{0:T(256)S(1)}, f32[201]{0:T(256)S(1)}, u32[]{:S(2)}, u32[]{:S(2)}) collective-permute-start(f32[201]{0:T(256)S(1)} %pad_maximum_fusion.32), channel_id=1, source_target_pairs={{0,2},{1,3},{2,0},{3,1},{4,6},{5,7},{6,4},{7,5},{8,10},{9,11},{10,... | collective-permute-start | bytes 2420 | tf_op jit(solution)/shard_map/ppermute | solution.py:51
  230.3 5.5 %collective-permute-start.41 = (f32[201]{0:T(256)S(1)}, f32[201]{0:T(256)S(1)}, u32[]{:S(2)}, u32[]{:S(2)}) collective-permute-start(f32[201]{0:T(256)S(1)} %pad_maximum_fusion.32), channel_id=1, source_target_pairs={{0,3},{1,2},{2,1},{3,0},{4,7},{5,6},{6,5},{7,4},{8,11},{9,10},{10,... | collective-permute-start | bytes 2420 | tf_op jit(solution)/shard_map/ppermute | solution.py:51
  243.2 3.7 collective-permute-start.43
  243.6 3.6 collective-permute-start.44
  244.9 3.1 collective-permute-start.45
  245.2 15.7 %collective-permute-start.47 = (bf16[200,800]{1,0:T(8,128)(2,1)S(1)}, bf16[200,800]{1,0:T(8,128)(2,1)S(1)}, u32[]{:S(2)}, u32[]{:S(2)}) collective-permute-start(bf16[200,800]{1,0:T(8,128)(2,1)S(1)} %dynamic-slice_convert_fusion.3), channel_id=1, source_target_pairs={{0,2},{1,3},{2,0},{3,1},{4,6},{5,7},{6,4},{7,5},{8,10},{9,11},{10,... | collective-permute-start | bytes 960008 | tf_op jit(solution)/shard_map/ppermute | solution.py:51
  246.5 15.2 %collective-permute-start.46 = (f32[160,800]{1,0:T(8,128)S(1)}, f32[160,800]{1,0:T(8,128)S(1)}, u32[]{:S(2)}, u32[]{:S(2)}) collective-permute-start(f32[160,800]{1,0:T(8,128)S(1)} %constant_dynamic-slice_fusion.2), channel_id=1, source_target_pairs={{0,1},{1,0},{2,3},{3,2},{4,5},{5,4},{6,7},{7,6},{8,9},{9,8},{10,11... | collective-permute-start | bytes 1536008 | tf_op jit(solution)/shard_map/ppermute | solution.py:51
  265.2 4.1 collective-permute-start.48
  265.3 4.0 collective-permute-start.49
  267.5 3.1 collective-permute-start.50
  267.6 40.0 %collective-permute-start.56 = (bf16[200,800]{1,0:T(8,128)(2,1)}, bf16[200,800]{1,0:T(8,128)(2,1)}, u32[]{:S(2)}, u32[]{:S(2)}) collective-permute-start(bf16[200,800]{1,0:T(8,128)(2,1)} %reduce-precision_convert_fusion.1), channel_id=1, source_target_pairs={{0,2},{1,3},{2,0},{3,1},{4,6},{5,7},{6,4},{7,5},{8,10},{9,11},{10,... | collective-permute-start | bytes 960008 | tf_op jit(solution)/shard_map/ppermute | solution.py:51
  272.2 4.2 collective-permute-start.51
  272.5 19.2 %collective-permute-start.52 = (f32[56,800]{1,0:T(8,128)S(1)}, f32[56,800]{1,0:T(8,128)S(1)}, u32[]{:S(2)}, u32[]{:S(2)}) collective-permute-start(f32[56,800]{1,0:T(8,128)S(1)} %get-tuple-element.266), channel_id=1, source_target_pairs={{0,2},{1,3},{2,0},{3,1},{4,6},{5,7},{6,4},{7,5},{8,10},{9,11},{10,... | collective-permute-start | bytes 537608 | tf_op jit(solution)/shard_map/ppermute | solution.py:51
  272.9 27.0 %collective-permute-start.53 = (f32[56,800]{1,0:T(8,128)S(1)}, f32[56,800]{1,0:T(8,128)S(1)}, u32[]{:S(2)}, u32[]{:S(2)}) collective-permute-start(f32[56,800]{1,0:T(8,128)S(1)} %get-tuple-element.265), channel_id=1, source_target_pairs={{0,3},{1,2},{2,1},{3,0},{4,7},{5,6},{6,5},{7,4},{8,11},{9,10},{10,... | collective-permute-start | bytes 537608 | tf_op jit(solution)/shard_map/ppermute | solution.py:51
  274.9 31.6 %collective-permute-start.55 = (f32[80,800]{1,0:T(8,128)}, f32[80,800]{1,0:T(8,128)}, u32[]{:S(2)}, u32[]{:S(2)}) collective-permute-start(f32[80,800]{1,0:T(8,128)} %constant_dynamic-slice_fusion.1), channel_id=1, source_target_pairs={{0,2},{1,3},{2,0},{3,1},{4,6},{5,7},{6,4},{7,5},{8,10},{9,11},{10,... | collective-permute-start | bytes 768008 | tf_op jit(solution)/shard_map/ppermute | solution.py:51
  276.4 32.4 %collective-permute-start.54 = (bf16[400,800]{1,0:T(8,128)(2,1)}, bf16[400,800]{1,0:T(8,128)(2,1)}, u32[]{:S(2)}, u32[]{:S(2)}) collective-permute-start(bf16[400,800]{1,0:T(8,128)(2,1)} %dynamic-slice_convert_fusion), channel_id=1, source_target_pairs={{0,1},{1,0},{2,3},{3,2},{4,5},{5,4},{6,7},{7,6},{8,9},{9,8},{10,11... | collective-permute-start | bytes 1920008 | tf_op jit(solution)/shard_map/ppermute | solution.py:51
  310.1 9.8 %collective-permute-start.59 = (f32[80,800]{1,0:T(8,128)S(1)}, f32[80,800]{1,0:T(8,128)S(1)}, u32[]{:S(2)}, u32[]{:S(2)}) collective-permute-start(f32[80,800]{1,0:T(8,128)S(1)} %dynamic-slice_add_fusion.1), channel_id=1, source_target_pairs={{0,2},{1,3},{2,0},{3,1},{4,6},{5,7},{6,4},{7,5},{8,10},{9,11},{10,... | collective-permute-start | bytes 768008 | tf_op jit(solution)/shard_map/ppermute | solution.py:51
  313.8 12.5 %collective-permute-start.57 = (bf16[400,800]{1,0:T(8,128)(2,1)S(1)}, bf16[400,800]{1,0:T(8,128)(2,1)S(1)}, u32[]{:S(2)}, u32[]{:S(2)}) collective-permute-start(bf16[400,800]{1,0:T(8,128)(2,1)S(1)} %bitcast.258), channel_id=1, source_target_pairs={{0,1},{1,0},{2,3},{3,2},{4,5},{5,4},{6,7},{7,6},{8,9},{9,8},{10,11... | collective-permute-start | bytes 1920008 | tf_op jit(solution)/shard_map/ppermute | solution.py:51
  313.9 12.3 %collective-permute-start.58 = (bf16[200,800]{1,0:T(8,128)(2,1)S(1)}, bf16[200,800]{1,0:T(8,128)(2,1)S(1)}, u32[]{:S(2)}, u32[]{:S(2)}) collective-permute-start(bf16[200,800]{1,0:T(8,128)(2,1)S(1)} %dynamic-slice_convert_fusion.2), channel_id=1, source_target_pairs={{0,2},{1,3},{2,0},{3,1},{4,6},{5,7},{6,4},{7,5},{8,10},{9,11},{10,... | collective-permute-start | bytes 960008 | tf_op jit(solution)/shard_map/ppermute | solution.py:51
  327.0 9.2 %collective-permute-start.60 = (bf16[200,800]{1,0:T(8,128)(2,1)S(1)}, bf16[200,800]{1,0:T(8,128)(2,1)S(1)}, u32[]{:S(2)}, u32[]{:S(2)}) collective-permute-start(bf16[200,800]{1,0:T(8,128)(2,1)S(1)} %reduce-precision_convert_fusion), channel_id=1, source_target_pairs={{0,2},{1,3},{2,0},{3,1},{4,6},{5,7},{6,4},{7,5},{8,10},{9,11},{10,... | collective-permute-start | bytes 960008 | tf_op jit(solution)/shard_map/ppermute | solution.py:51
  328.7 9.2 %collective-permute-start.62 = (f32[160,800]{1,0:T(8,128)S(1)}, f32[160,800]{1,0:T(8,128)}, u32[]{:S(2)}, u32[]{:S(2)}) collective-permute-start(f32[160,800]{1,0:T(8,128)S(1)} %bitcast.260), channel_id=1, source_target_pairs={{0,1},{1,0},{2,3},{3,2},{4,5},{5,4},{6,7},{7,6},{8,9},{9,8},{10,11... | collective-permute-start | bytes 1536008 | tf_op jit(solution)/shard_map/ppermute | solution.py:51
  375.3 17.5 %collective-permute-start.63 = (bf16[800,800]{1,0:T(8,128)(2,1)S(1)}, bf16[800,800]{1,0:T(8,128)(2,1)}, u32[]{:S(2)}, u32[]{:S(2)}) collective-permute-start(bf16[800,800]{1,0:T(8,128)(2,1)S(1)} %shard_map.400), channel_id=1, source_target_pairs={{0,1},{1,0},{2,3},{3,2},{4,5},{5,4},{6,7},{7,6},{8,9},{9,8},{10,11... | collective-permute-start | bytes 3840008 | tf_op jit(solution)/shard_map/ppermute | solution.py:51
  454.5 5.8 %collective-permute-start.64 = (bf16[224,800]{1,0:T(8,128)(2,1)S(1)}, bf16[224,800]{1,0:T(8,128)(2,1)S(1)}, u32[]{:S(2)}, u32[]{:S(2)}) collective-permute-start(bf16[224,800]{1,0:T(8,128)(2,1)S(1)} %shard_map.401), channel_id=1, source_target_pairs={{0,1},{1,0},{2,3},{3,2},{4,5},{5,4},{6,7},{7,6},{8,9},{9,8},{10,11... | collective-permute-start | bytes 1075208 | tf_op jit(solution)/shard_map/ppermute | solution.py:51
  (103 other events, 751.7 us)
Sparse Core Ops, SparseCore 0:
  109.0 57.7 all-gather.5
  224.6 89.1 all-gather.7
  337.3 56.4 all-gather.9
